TPU v7x, 256 devices: a whole 4x4x8 slice. The times are simulated.
256 devices in a mesh: row: 64 (over z, y, core), col: 4 (over x).
Axes of the slice: x: 4, y: 4, z: 8, core: 2. Of those that a mesh axis runs over, the one named last changes fastest.
Arguments:
- panel_col: float32 [131072, 256], P('row', 'col'), may hold values from -6 to 6
- look_cols: float32 [131072, 2048], P('row', 'col'), may hold values from -6 to 6
- sketch_map: float32 [256, 131072], P(None, 'row'), may hold values from -0.015625 to 0.015625
- upper_inv: float32 [256, 256], replicated, may hold values from -0.09375 to 0.09375
- lower_inv: float32 [256, 256], replicated, may hold values from -0.375 to 0.375
- pivots: int32 [256], replicated, may hold values from 256 to 131071, as said below
Outputs:
- l_panel: float32 [131072, 256], P('row', 'col')
- updated: float32 [131072, 2048], P('row', 'col')
- sketch: float32 [256, 256], P(None, 'col')
Inputs may be any that keep to these rules, and one draw needn't show every extreme that they name: `pivots`: distinct rows, none of them among the first 256.
All inputs are finite; a program needn't handle non-finite values.
Results may differ from a plain program's by a relative error of at most 0.000073.
Values sent between devices are 32-bit elements; how exact they have to be, the bound alone decides.
A program may use at most 64 MiB of HBM per device.

v0:
```python
import jax
import jax.numpy as jnp
from jax import lax
from jax.sharding import PartitionSpec as P

high_prec = lax.Precision.HIGHEST


def on_device(panel_col, look_cols, sketch_map, upper_inv, lower_inv, pivots):
    row_count = panel_col.shape[0]
    col_width = panel_col.shape[1]
    block_size = upper_inv.shape[0]
    col_index = lax.axis_index("col")
    row_index = lax.axis_index("row")
    first_row = row_index * row_count
    owned = (pivots >= first_row) & (pivots < first_row + row_count)
    local_idx = jnp.where(owned, pivots - first_row, 0)
    owned_mask = owned[:, None]
    panel_pick = jnp.where(owned_mask, panel_col[local_idx], 0.0)
    look_pick = jnp.where(owned_mask, look_cols[local_idx], 0.0)
    sketch_part = jnp.dot(
        sketch_map, panel_col, precision=high_prec, preferred_element_type=jnp.float32
    )
    on_root = row_index == 0
    panel_head = jnp.where(on_root, panel_col[:block_size], 0.0)
    look_head = jnp.where(on_root, look_cols[:block_size], 0.0)
    sketch, panel_piv, look_piv, panel_orig, look_orig = lax.psum(
        (sketch_part, panel_pick, look_pick, panel_head, look_head), "row"
    )
    target = jnp.where(owned, pivots - first_row, row_count)
    swapped_panel = panel_col.at[target].set(panel_orig, mode="drop")
    swapped_look = look_cols.at[target].set(look_orig, mode="drop")
    swapped_panel = jnp.where(on_root, swapped_panel.at[:block_size].set(panel_piv), swapped_panel)
    swapped_look = jnp.where(on_root, swapped_look.at[:block_size].set(look_piv), swapped_look)
    upper_tri = jnp.triu(upper_inv)
    lower_tri = jnp.tril(lower_inv, -1) + jnp.eye(block_size, dtype=jnp.float32)
    upper_rows = lax.dynamic_slice_in_dim(upper_tri, col_index * col_width, col_width, 0)
    partial_prod = jnp.dot(
        swapped_panel, upper_rows, precision=high_prec, preferred_element_type=jnp.float32
    )
    factor = lax.psum(partial_prod, "col")
    global_row = first_row + jnp.arange(row_count, dtype=jnp.int32)
    is_top = (global_row < block_size)[:, None]
    my_factor = lax.dynamic_slice_in_dim(factor, col_index * col_width, col_width, 1)
    l_panel = jnp.where(is_top, swapped_panel, my_factor)
    u_rows = jnp.dot(lower_tri, look_piv, precision=high_prec, preferred_element_type=jnp.float32)
    updated = swapped_look - jnp.dot(
        factor, u_rows, precision=high_prec, preferred_element_type=jnp.float32
    )
    updated = jnp.where(on_root, updated.at[:block_size].set(u_rows), updated)
    return (l_panel, updated, sketch)


def solution(mesh):
    placed = (P("row", "col"), P("row", "col"), P(None, "row"), P(), P(), P())
    return jax.shard_map(
        on_device,
        mesh=mesh,
        in_specs=placed,
        out_specs=(P("row", "col"), P("row", "col"), P(None, "col")),
        check_vma=False,
    )
```

profile of v0, /device:TPU:1, one launch (start us, length us, event | category | flops | bytes accessed | tf_op | source)
XLA Modules:
  0.0 307.5 jit_solution(13693479291795300407)
XLA Ops:
  7.2 0.0 copy-start
  7.2 0.0 copy-start.5
  7.2 0.0 all-reduce.6.cloned.1.call-start
  7.2 4.8 %copy.27 = f32[2048,512]{1,0:T(8,128)} copy(f32[2048,512]{1,0:T(8,128)} %param.13) | data formatting | bytes 8388608
  12.0 0.0 copy-done.5
  12.1 1.4 copy.10
  13.4 0.0 copy-done
  13.5 3.7 %fusion.14 = f32[256,64]{0,1:T(8,128)} fusion(f32[256,2048]{1,0:T(8,128)S(1)} %copy-done, f32[2048,64]{0,1:T(8,128)} %param.12), kind=kOutput, calls=%fused_computation.36 | convolution fusion | flops 402653184 | bytes 2686976 | tf_op jit(solution)/shard_map/dot_general | solution.py:21
  17.2 0.7 gather_fusion
  17.9 4.2 %gather_fusion.1 = f32[256,512]{1,0:T(8,128)} fusion(f32[2048,512]{1,0:T(8,128)} %copy.27, s32[1024]{0:T(1024)S(1)} %pad_clamp_fusion), kind=kCustom, calls=%fused_computation.1 | custom fusion | bytes 1049600 | tf_op jit(solution)/shard_map/gather | solution.py:20
  22.1 0.7 slice_select_fusion.4
  22.8 2.3 slice_select_fusion.2
  25.1 0.0 all-reduce.6.cloned.1.call-update
  25.1 0.0 all-reduce.4.cloned.1.call-start
  25.2 0.1 iota_compare_fusion.1
  25.3 190.4 %all-reduce.6.cloned.1.call-done = (f32[256,64]{1,0:T(8,128)}, f32[256,64]{1,0:T(8,128)}, f32[256,512]{1,0:T(8,128)}, f32[256,512]{1,0:T(8,128)}, f32[256,64]{0,1:T(8,128)}) async-done(((f32[256,64]{1,0:T(8,128)}, f32[256,64]{1,0:T(8,128)}, f32[256,512]{1,0:T(8,128)}, f32[256,512]{1,0:T(8,128)}, f32[256,64]{0,1:T(8,128)}), (f32[256,64]{1,0:T(8,128)}, f32[256,64]{1,0:T(8,128)}, f32[256,512]{1,0:T(8,128)}, ...) | async-done | bytes 1245200 | tf_op jit(solution)/shard_map/psum | solution.py:27
  215.7 1.9 scatter_fusion
  217.7 3.9 %fusion.8 = f32[2048,256]{1,0:T(8,128)} fusion(f32[2048,64]{1,0:T(8,128)S(1)} %fusion.6, f32[256,256]{1,0:T(8,128)} %param.15, s32[]{:T(128)S(6)} %select_n.87, pred[256,256]{1,0:T(32,128)(4,1)S(1)} %iota_compare_fusion.1), kind=kOutput, calls=%fused_computation.23 | convolution fusion | flops 402669568 | bytes 3227652 | tf_op jit(solution)/shard_map/dot_general | solution.py:38
  221.6 0.0 all-reduce.4.cloned.1.call-update
  221.7 0.0 copy-start.3
  221.7 6.1 %scatter_fusion.1 = f32[2048,512]{1,0:T(8,128)} fusion(f32[2048,512]{1,0:T(8,128)} %copy.27, s32[256]{0:T(256)S(1)} %get-tuple-element.48, f32[256,512]{1,0:T(8,128)} %get-tuple-element.44), kind=kCustom, calls=%fused_computation.3 | custom fusion | bytes 1573888 | tf_op jit(solution)/shard_map/scatter | solution.py:32
  227.8 0.0 copy-done.3
  227.8 2.5 fusion.2
  230.3 1.9 fusion.1
  232.2 53.3 %all-reduce.4.cloned.1.call-done = f32[2048,256]{1,0:T(8,128)} async-done(((f32[2048,256]{1,0:T(8,128)}), f32[2048,256]{1,0:T(8,128)}) %all-reduce.4.cloned.1.call-update) | async-done | bytes 2097168 | tf_op jit(solution)/shard_map/psum | solution.py:41
  285.5 0.0 copy-start.2
  285.5 0.0 copy-start.1
  285.5 8.7 %convolution_subtract_fusion = f32[2048,512]{1,0:T(8,128)} fusion(f32[2048,512]{1,0:T(8,128)} %fusion.1, f32[2048,256]{1,0:T(8,128)} %all-reduce.4.cloned.1.call-done, f32[256,512]{1,0:T(8,128)} %fusion.2), kind=kOutput, calls=%fused_computation.4 | convolution fusion | flops 3222274048 | bytes 11010048 | tf_op jit(solution)/shard_map/dot_general | solution.py:47
  294.1 0.0 copy-done.2
  294.1 0.0 copy-start.4
  294.1 1.9 fusion
  296.1 0.0 copy-done.1
  296.1 1.6 dynamic-slice_select_fusion
  297.7 2.3 copy.12
  300.0 0.0 copy-done.4
  300.0 0.6 copy.28
  (6 shorter events, 0.1 us)
Async XLA Ops:
  7.2 6.3 %copy-start = (f32[256,2048]{1,0:T(8,128)S(1)}, f32[256,2048]{1,0:T(8,128)}, u32[]{:S(2)}) copy-start(f32[256,2048]{1,0:T(8,128)} %param.14) | copy-start | bytes 6291460
  7.2 4.8 %copy-start.5 = (s32[256]{0:T(256)S(1)}, s32[256]{0:T(256)}, u32[]{:S(2)}) copy-start(s32[256]{0:T(256)} %param.17) | copy-start | bytes 3076
  7.2 208.5 %all-reduce.6.cloned.1.call-start = ((), (), s32[]{:S(2)}) async-start(), calls=%async_computation.1 | async-start | bytes 2752512 | tf_op jit(solution)/shard_map/psum | solution.py:27
  25.1 260.4 %all-reduce.4.cloned.1.call-start = ((), (), s32[]{:S(2)}) async-start(), calls=%async_computation | async-start | bytes 4194304 | tf_op jit(solution)/shard_map/psum | solution.py:41
  221.7 6.1 %copy-start.3 = (f32[256,256]{1,0:T(8,128)S(1)}, f32[256,256]{1,0:T(8,128)}, u32[]{:S(2)}) copy-start(f32[256,256]{1,0:T(8,128)} %param.16) | copy-start | bytes 786436
  285.5 8.7 %copy-start.2 = (f32[256,512]{1,0:T(8,128)S(1)}, f32[256,512]{1,0:T(8,128)}, u32[]{:S(2)}) copy-start(f32[256,512]{1,0:T(8,128)} %fusion.2) | copy-start | bytes 1572868
  285.5 10.6 %copy-start.1 = (f32[2048,256]{1,0:T(8,128)S(1)}, f32[2048,256]{1,0:T(8,128)}, u32[]{:S(2)}) copy-start(f32[2048,256]{1,0:T(8,128)} %all-reduce.4.cloned.1.call-done) | copy-start | bytes 6291460
  294.1 5.9 %copy-start.4 = (f32[256,64]{0,1:T(8,128)S(1)}, f32[256,64]{0,1:T(8,128)}, u32[]{:S(2)}) copy-start(f32[256,64]{0,1:T(8,128)} %get-tuple-element.55) | copy-start | bytes 196612
Sparse Core Ops, SparseCore 0:
  25.2 190.4 all-reduce.5
  221.8 63.6 all-reduce.3
where the time goes:
time: 308 us; the launch traced here: 307 us
  waiting for transfers between devices  244 us (79%)
  local copies, waits for them, and re-layouts  22.1 us (7%)
  matrix products  18.8 us (6%)
  between operations  14.2 us (5%)
  other arithmetic  8.61 us (3%)
    psum x1, waiting for transfers between devices, on_device(): lax.psum((sketch_part, panel_pick, look_pick, panel_head, look_head), 'row')  190 us
    psum x1, waiting for transfers between devices, on_device(): factor = lax.psum(partial_prod, 'col')  53.3 us
    unnamed x16, local copies, waits for them, and re-layouts  9.15 us
    dot_general x1, matrix products, on_device(): jnp.dot(factor, u_rows, precision=high_prec, preferred_element_type=jnp.f...  8.65 us
  transfers between devices with their start and end apart: 2, of which 2 were waited for; matrix products, arithmetic and copies ran while one was open for 3% of the time, Pallas kernels for 0%

commit v1 on v0

v1 whole, which is shorter than its diff:
```python
import jax
import jax.numpy as jnp
from jax import lax
from jax.experimental import pallas as pl
from jax.experimental.pallas import tpu as pltpu
from jax.sharding import PartitionSpec as P

MESH = pl.DeviceIdType.MESH
F32, BF16 = jnp.float32, jnp.bfloat16
NB = 256
CY, CZ = 4, 8

X_RING = 0
A_CORE = 6
A_Y = 10
A_Z = 13
A_GZ = 20
A_GY = 27
A_GC = 30
S_CORE = 34
S_Z = 35
S_Y = 42
S_GZ = 45
S_GC = 52
H_X = 53
H_Z = 56
H_Y = 63
H_GZ = 66
H_GY = 73
H_GC = 76
N_SEM = 77


def split(a):
    hi = a.astype(BF16)
    return hi, (a - hi.astype(F32)).astype(BF16)


def dot(a, b, dims=((1,), (0,))):
    return lax.dot_general(a, b, (dims, ((), ())), preferred_element_type=F32)


def dot3(a, b, dims=((1,), (0,))):
    (ah, al), (bh, bl) = a, b
    return dot(ah, bh, dims) + dot(al, bh, dims) + dot(ah, bl, dims)


def comm_kernel(
    piv_s, piv_v, panel, look, smap,
    piv, head, red, ph, plo,
    look_v, sm_v, gath, pick, cbuf, hsum, ybuf, zin, zbuf,
    spart, scbuf, ssum, szbuf, sybuf, deal,
    ld, ss, rs,
):
    r, x = lax.axis_index("row"), lax.axis_index("col")
    c = lax.rem(r, 2)
    y = lax.rem(lax.div(r, 2), CY)
    z = lax.div(r, 2 * CY)
    first = r * look.shape[0]
    root = r == 0

    def to_x(d):
        return (r, lax.rem(x + d + 4, 4))

    def to_y(d):
        return ((z * CY + lax.rem(y + d, CY)) * 2 + c, x)

    def to_z(d):
        return ((lax.rem(z + d, CZ) * CY + y) * 2 + c, x)

    sibling = ((z * CY + y) * 2 + 1 - c, x)

    pending = []

    def remote(src, dst, slot, device, recv_slot=None):
        return pltpu.make_async_remote_copy(
            src_ref=src, dst_ref=dst, send_sem=ss.at[slot],
            recv_sem=rs.at[slot if recv_slot is None else recv_slot],
            device_id=device, device_id_type=MESH,
        )

    def send(*args):
        copy = remote(*args)
        copy.start()
        pending.append(copy)
        return copy

    def rows8(i):
        return pl.ds(pl.multiple_of(i * 8, 8), 8)

    def rows64(i):
        return pl.ds(pl.multiple_of(i * 64, 64), 64)

    mine = pl.ds(pl.multiple_of(c * 256, 256), 256)
    other = pl.ds(pl.multiple_of((1 - c) * 256, 256), 256)
    half_cols = gath.shape[1] // 2
    halves = [pl.ds(0, half_cols), pl.ds(half_cols, half_cols)]
    own_block = rows64(x)

    load_look = pltpu.make_async_copy(look, look_v, ld.at[0])
    load_look.start()
    load_panel = pltpu.make_async_copy(panel, gath.at[own_block, :], ld.at[1])
    load_panel.start()
    load_map = pltpu.make_async_copy(smap, sm_v, ld.at[2])
    load_map.start()

    bar = pltpu.get_barrier_semaphore()
    partners = [to_x(d) for d in (1, 2, 3)] + [to_y(d) for d in range(1, CY)]
    partners += [to_z(d) for d in range(1, CZ)] + [sibling]
    for device in partners:
        pl.semaphore_signal(bar, inc=1, device_id=device, device_id_type=MESH)

    load_look.wait()

    def pick_rows(i, carry):
        for k in range(8):
            row = i * 8 + k
            local = piv_s[row] - first
            owned = (local >= 0) & (local < look_v.shape[0])
            at = jnp.where(owned, local, 0)
            pick[pl.ds(row, 1), :] = jnp.where(owned, look_v[pl.ds(at, 1), :], 0.0)
        return carry

    lax.fori_loop(0, NB // 8, pick_rows, 0)
    pl.semaphore_wait(bar, len(partners))

    a_core = []
    for d in (1, 2, 3, 0):
        block = rows64(lax.rem(y + d, CY))
        a_core.append((d, block, send(pick.at[block, other], cbuf.at[block, :], A_CORE + d, sibling)))

    right, left = to_x(1), to_x(-1)
    ring = [
        send(panel.at[:, halves[0]], gath.at[own_block, halves[0]], X_RING, right),
        send(panel.at[:, halves[1]], gath.at[own_block, halves[1]], X_RING + 2, left),
        send(panel.at[:, halves[1]], gath.at[own_block, halves[1]], X_RING + 1, right),
        send(panel.at[:, halves[0]], gath.at[own_block, halves[0]], X_RING + 3, left),
    ]

    @pl.when(root)
    def _():
        local = [pltpu.make_async_copy(panel.at[:, pl.ds(0, NB)], deal.at[x, :, pl.ds(512, NB)], ld.at[3])]
        for q in range(CY):
            local.append(
                pltpu.make_async_copy(look.at[pl.ds(64 * q, 64), :], deal.at[q, :, pl.ds(0, 512)], ld.at[4 + q])
            )
        for copy in local:
            copy.start()
        sends = []
        for d in (1, 2, 3):
            sends.append(
                remote(panel.at[:, pl.ds(0, NB)], deal.at[x, :, pl.ds(512, NB)], H_X + d - 1, to_x(d))
            )
            sends[-1].start()
        for copy in local:
            copy.wait()
        for copy in sends:
            copy.wait()

    a_y = []
    for d, block, copy in a_core:
        copy.wait_recv()
        hsum[block, :] = pick[block, mine] + cbuf[block, :]
        if d:
            a_y.append(send(hsum.at[block, :], ybuf.at[d - 1], A_Y + d - 1, to_y(d)))

    @pl.when(root)
    def _():
        for d in range(1, CZ):
            remote(deal.at[:, pl.ds(8 * d, 8), :], deal.at[:, pl.ds(8 * d, 8), :], H_Z + d - 1, to_z(d), H_Z).start()

    load_panel.wait()
    load_map.wait()
    spart[...] = jnp.zeros_like(spart)
    tile = 512

    def small(i, carry):
        cols = pl.ds(pl.multiple_of(i * tile, tile), tile)
        p = gath[own_block, cols]
        p1, p2 = split(p)
        p3 = (p - p1.astype(F32) - p2.astype(F32)).astype(BF16)
        mh, ml = split(sm_v[:, cols])
        nt = ((1,), (1,))
        both = dot(jnp.concatenate([p1, p2], 0), mh, nt)
        spart[0:64, :] += both[0:64] + both[64:128] + dot(p1, ml, nt)
        at = lax.broadcasted_iota(jnp.int32, (tile, NB), 0) + (first + i * tile)
        hot = jnp.where(at == piv_v[...], 1.0, 0.0).astype(BF16)
        three = dot(jnp.concatenate([p1, p2, p3], 0), hot)
        spart[64:128, :] += three[0:64] + three[64:128] + three[128:192]
        return carry

    lax.fori_loop(0, gath.shape[1] // tile, small, 0)
    s_core = send(spart.at[rows64(1 - c), :], scbuf, S_CORE, sibling)

    for copy in a_y:
        copy.wait_recv()
    zin[...] = hsum[rows64(y), :] + ybuf[0] + ybuf[1] + ybuf[2]
    a_z = [send(zin.at[rows8(lax.rem(z + d, CZ)), :], zbuf.at[d - 1], A_Z + d - 1, to_z(d)) for d in range(1, CZ)]

    my_head = head.at[y, rows8(z), :]

    @pl.when((y == 0) & (c == 0))
    def _():
        @pl.when(z > 0)
        def _():
            landed = deal.at[:, rows8(z), :]
            remote(landed, landed, H_Z, to_z(1)).wait_recv()

        for d in range(1, CY):
            remote(deal.at[d, rows8(z), :], head.at[d, rows8(z), :], H_Y + d - 1, to_y(d), H_Y).start()
        head[0, rows8(z), :] = deal[0, rows8(z), :]

    s_core.wait_recv()
    ssum[...] = spart[rows64(c), :] + scbuf[...]
    s_z = [send(ssum.at[rows8(lax.rem(z + d, CZ)), :], szbuf.at[d - 1], S_Z + d - 1, to_z(d)) for d in range(1, CZ)]

    @pl.when(c == 0)
    def _():
        @pl.when(y > 0)
        def _():
            remote(my_head, my_head, H_Y, to_y(1)).wait_recv()

        for d in range(1, CZ):
            remote(my_head, my_head, H_GZ + d - 1, to_z(d)).start()

    ring[0].wait_recv()
    block = gath.at[rows64(lax.rem(x + 3, 4)), halves[0]]
    ring.append(send(block, block, X_RING + 4, right))
    ring[1].wait_recv()
    block = gath.at[rows64(lax.rem(x + 1, 4)), halves[1]]
    ring.append(send(block, block, X_RING + 5, left))

    for copy in a_z:
        copy.wait_recv()
    at_mine = pl.ds(pl.multiple_of(y * 64 + z * 8, 8), 8)
    total = zin[rows8(z), :]
    for d in range(1, CZ):
        total = total + zbuf[d - 1]
    piv[at_mine, mine] = total
    chunk = piv.at[at_mine, mine]
    a_gz = [send(chunk, chunk, A_GZ + d - 1, to_z(d)) for d in range(1, CZ)]

    @pl.when(c == 0)
    def _():
        for d in range(1, CZ):
            remote(my_head, my_head, H_GZ + d - 1, to_z(d)).wait_recv()
        for d in range(1, CY):
            remote(head.at[y], head.at[y], H_GY + d - 1, to_y(d)).start()

    for copy in s_z:
        copy.wait_recv()
    total = ssum[rows8(z), :]
    for d in range(1, CZ):
        total = total + szbuf[d - 1]
    sybuf[y] = total
    s_y = [send(sybuf.at[y], sybuf.at[y], S_Y + d - 1, to_y(d)) for d in range(1, CY)]

    for copy in a_gz:
        copy.wait_recv()
    quarter = piv.at[rows64(y), mine]
    a_gy = [send(quarter, quarter, A_GY + d - 1, to_y(d)) for d in range(1, CY)]
    a_gc = [send(quarter, quarter, A_GC, sibling)]

    for copy in s_y:
        copy.wait_recv()
    at_small = pl.ds(pl.multiple_of(c * 64 + z * 8, 8), 8)
    red[at_small, :] = sybuf[0] + sybuf[1] + sybuf[2] + sybuf[3]
    s_gz = [send(red.at[at_small, :], red.at[at_small, :], S_GZ + d - 1, to_z(d)) for d in range(1, CZ)]

    @pl.when(c == 0)
    def _():
        for d in range(1, CY):
            remote(head.at[y], head.at[y], H_GY + d - 1, to_y(d)).wait_recv()
        remote(head, head, H_GC, sibling).start()

    for copy in ring[2:]:
        copy.wait_recv()

    def turn(i, carry):
        at = pl.ds(pl.multiple_of(i * 256, 256), 256)
        hi, lo = split(gath[:, at].T)
        ph[at, :] = hi
        plo[at, :] = lo
        return carry

    lax.fori_loop(0, gath.shape[1] // 256, turn, 0)

    for d, copy in zip(range(1, CY), a_gy):
        copy.wait_recv()
        block = piv.at[rows64(lax.rem(y + CY - d, CY)), mine]
        a_gc.append(send(block, block, A_GC + d, sibling))

    for copy in s_gz:
        copy.wait_recv()
    s_gc = send(red.at[rows64(c), :], red.at[rows64(c), :], S_GC, sibling)
    for copy in a_gc:
        copy.wait_recv()
    s_gc.wait_recv()

    @pl.when(c == 1)
    def _():
        remote(head, head, H_GC, sibling).wait_recv()

    for copy in pending:
        copy.wait_send()

    @pl.when(c == 0)
    def _():
        remote(head, head, H_GC, sibling).wait_send()
        for d in range(1, CZ):
            remote(my_head, my_head, H_GZ + d - 1, to_z(d)).wait_send()
        for d in range(1, CY):
            remote(head.at[y], head.at[y], H_GY + d - 1, to_y(d)).wait_send()

    @pl.when((y == 0) & (c == 0))
    def _():
        for d in range(1, CY):
            remote(deal.at[d, rows8(z), :], head.at[d, rows8(z), :], H_Y + d - 1, to_y(d)).wait_send()

    @pl.when(root)
    def _():
        for d in range(1, CZ):
            part = deal.at[:, pl.ds(8 * d, 8), :]
            remote(part, part, H_Z + d - 1, to_z(d)).wait_send()


def update_kernel(
    info, piv_v, look, ph, plo, piv, head, red, upper, lower,
    out, lp, sk,
    vh, vl, th, tl, ut, uh, ul, fh, fl, ur,
):
    step = pl.program_id(0)
    tile = look.shape[0]
    first, x = info[0], info[1]

    @pl.when(step == 0)
    def _():
        i = lax.broadcasted_iota(jnp.int32, (NB, NB), 0)
        j = lax.broadcasted_iota(jnp.int32, (NB, NB), 1)
        low = jnp.where(i > j, lower[...], jnp.where(i == j, 1.0, 0.0))
        up = jnp.where(i <= j, upper[...], 0.0)
        u_rows = dot3(split(low), split(piv[...]))
        ur[...] = u_rows
        v = split(dot3(split(up), split(u_rows)))
        vh[...], vl[...] = v
        rows = head[...].reshape(NB, 768)
        cols = split(rows[:, 512:])
        t = rows[:, :512] - dot3(split(rows[:, 512:].T), v)
        th[...], tl[...] = split(t)
        ut[...] = up.T
        u = split(ut[pl.ds(pl.multiple_of(x * 64, 64), 64), :])
        uh[...], ul[...] = u
        fh[...], fl[...] = split(dot3(u, cols))
        sk[...] = red[0:64, :]

    at = lax.broadcasted_iota(jnp.int32, (tile, NB), 0) + (first + step * tile)
    hot32 = jnp.where(at == piv_v[...], 1.0, 0.0)
    hit = jnp.max(hot32, axis=1, keepdims=True)
    hot = hot32.astype(BF16)
    p = (ph[...], plo[...])
    plain = look[...] - dot3(p, (vh[...], vl[...]))
    moved = dot(hot, th[...]) + dot(hot, tl[...])
    out[...] = jnp.where(hit > 0.0, moved, plain)
    nt = ((1,), (1,))
    factor = dot3((uh[...], ul[...]), p, nt)
    parts = dot(jnp.concatenate([fh[...], fl[...], jnp.ones((16, NB), BF16)], 0), hot, nt)
    lp[...] = jnp.where(parts[128:129] > 0.0, parts[0:64] + parts[64:128], factor)

    @pl.when((step == 0) & (first == 0))
    def _():
        out[0:NB, :] = ur[...]
        lp[:, 0:NB] = red[64:128, :]


def on_device(panel_col, look_cols, sketch_map, upper_inv, lower_inv, pivots):
    rows, width = look_cols.shape
    panel_t = panel_col.T
    piv_row = pivots.reshape(1, NB)
    vmem = pl.BlockSpec(memory_space=pltpu.VMEM)
    smem = pl.BlockSpec(memory_space=pltpu.SMEM)
    hbm = pl.BlockSpec(memory_space=pl.ANY)
    piv, head, red, ph, plo = pl.pallas_call(
        comm_kernel,
        out_shape=(
            jax.ShapeDtypeStruct((NB, width), F32),
            jax.ShapeDtypeStruct((CY, 64, width + NB), F32),
            jax.ShapeDtypeStruct((128, NB), F32),
            jax.ShapeDtypeStruct((rows, NB), BF16),
            jax.ShapeDtypeStruct((rows, NB), BF16),
        ),
        in_specs=[smem, vmem, hbm, hbm, hbm],
        out_specs=(vmem,) * 5,
        scratch_shapes=[
            pltpu.VMEM((rows, width), F32),
            pltpu.VMEM((NB, rows), F32),
            pltpu.VMEM((NB, rows), F32),
            pltpu.VMEM((NB, width), F32),
            pltpu.VMEM((NB, 256), F32),
            pltpu.VMEM((NB, 256), F32),
            pltpu.VMEM((3, 64, 256), F32),
            pltpu.VMEM((64, 256), F32),
            pltpu.VMEM((7, 8, 256), F32),
            pltpu.VMEM((128, NB), F32),
            pltpu.VMEM((64, NB), F32),
            pltpu.VMEM((64, NB), F32),
            pltpu.VMEM((7, 8, NB), F32),
            pltpu.VMEM((4, 8, NB), F32),
            pltpu.VMEM((CY, 64, width + NB), F32),
            pltpu.SemaphoreType.DMA((8,)),
            pltpu.SemaphoreType.DMA((N_SEM,)),
            pltpu.SemaphoreType.DMA((N_SEM,)),
        ],
        compiler_params=pltpu.CompilerParams(
            collective_id=0, has_side_effects=True, vmem_limit_bytes=40 << 20
        ),
        name="exchange",
    )(pivots, piv_row, panel_t, look_cols, sketch_map)

    info = jnp.stack([lax.axis_index("row") * rows, lax.axis_index("col")]).astype(jnp.int32)
    tile = 512

    def whole(shape):
        return pl.BlockSpec(shape, lambda i: (0,) * len(shape))

    def by_row(cols):
        return pl.BlockSpec((tile, cols), lambda i: (i, 0))

    updated, lp, sk = pl.pallas_call(
        update_kernel,
        grid=(rows // tile,),
        out_shape=(
            jax.ShapeDtypeStruct((rows, width), F32),
            jax.ShapeDtypeStruct((64, rows), F32),
            jax.ShapeDtypeStruct((64, NB), F32),
        ),
        in_specs=[
            smem, whole((1, NB)), by_row(width), by_row(NB), by_row(NB),
            whole((NB, width)), whole((CY, 64, width + NB)), whole((128, NB)), whole((NB, NB)), whole((NB, NB)),
        ],
        out_specs=(by_row(width), pl.BlockSpec((64, tile), lambda i: (0, i)), whole((64, NB))),
        scratch_shapes=[
            pltpu.VMEM((NB, width), BF16),
            pltpu.VMEM((NB, width), BF16),
            pltpu.VMEM((NB, width), BF16),
            pltpu.VMEM((NB, width), BF16),
            pltpu.VMEM((NB, NB), F32),
            pltpu.VMEM((64, NB), BF16),
            pltpu.VMEM((64, NB), BF16),
            pltpu.VMEM((64, NB), BF16),
            pltpu.VMEM((64, NB), BF16),
            pltpu.VMEM((NB, width), F32),
        ],
        compiler_params=pltpu.CompilerParams(vmem_limit_bytes=32 << 20),
        name="update",
    )(info, piv_row, look_cols, ph, plo, piv, head, red, upper_inv, lower_inv)
    return lp.T, updated, sk.T


def solution(mesh):
    placed = (P("row", "col"), P("row", "col"), P(None, "row"), P(), P(), P())
    return jax.shard_map(
        on_device,
        mesh=mesh,
        in_specs=placed,
        out_specs=(P("row", "col"), P("row", "col"), P(None, "col")),
        check_vma=False,
    )
```

time: 308 us -> 71.3 us (0.23)
  waiting for transfers between devices: 244 us -> 0 us
  Pallas kernels: 0 us -> 64.8 us
  matrix products: 18.8 us -> 0 us
  local copies, waits for them, and re-layouts: 22.1 us -> 5.51 us
  between operations: 14.2 us -> 0.66 us
  other arithmetic: 8.61 us -> 0.08 us
    psum x2 -> x0, waiting for transfers between devices: 244 us -> none  [the longest x1 190 us: on_device(): lax.psum((sketch_part, panel_pick, look_pick, panel_head, look_head), 'row')]
    pallas_call x0 -> x2, Pallas kernels: none -> 64.8 us  [the longest x1 57.3 us: on_device(): pl.pallas_call(comm_kernel, out_shape=(jax.ShapeDtypeStruct((NB, width),...]
    dot_general x4 -> x0, matrix products: 18.8 us -> none  [the longest x1 8.65 us: on_device(): jnp.dot(factor, u_rows, precision=high_prec, preferred_element_type=jnp.f...]
    select_n x7 -> x0, other arithmetic: 8.48 us -> none  [the longest x1 2.25 us: on_device(): look_head = jnp.where(on_root, look_cols[:block_size], 0.0)]
    scatter x2 -> x0, local copies, waits for them, and re-layouts: 8.03 us -> none  [the longest x1 6.12 us: on_device(): swapped_look = look_cols.at[target].set(look_orig, mode='drop')]
    gather x2 -> x0, local copies, waits for them, and re-layouts: 4.91 us -> none  [the longest x1 4.18 us: on_device(): look_pick = jnp.where(owned_mask, look_cols[local_idx], 0.0)]
    unnamed x16 -> x12, local copies, waits for them, and re-layouts: 9.15 us -> 5.51 us
  transfers between devices with their start and end apart: 2 -> 0, of which waited for: 2 -> 0; matrix products, arithmetic and copies ran while one was open for 3% -> 0% of each run, Pallas kernels for 0% -> 0%
where the time goes in v1:
time: 71.3 us; the launch traced here: 71.1 us
  Pallas kernels  64.8 us (91%)
  local copies, waits for them, and re-layouts  5.51 us (8%)
    pallas_call x1, Pallas kernels, on_device(): pl.pallas_call(comm_kernel, out_shape=(jax.ShapeDtypeStruct((NB, width),...  57.3 us
    pallas_call x1, Pallas kernels, on_device(): pl.pallas_call(update_kernel, grid=(rows // tile,), out_shape=(jax.ShapeD...  7.55 us
    unnamed x12, local copies, waits for them, and re-layouts  5.51 us

profile of v1, /device:TPU:1, one launch (start us, length us, event | category | flops | bytes accessed | tf_op | source)
XLA Modules:
  0.0 71.1 jit_solution(10742709244453525071)
XLA Ops:
  0.6 0.1 pad_add_fusion.info
  0.7 0.0 copy-start
  0.7 2.2 %copy-done = f32[2048,512]{1,0:T(8,128)S(1)} copy-done((f32[2048,512]{1,0:T(8,128)S(1)}, f32[2048,512]{1,0:T(8,128)}, u32[]{:S(2)}) %copy-start) | copy-done | bytes 4194328
  2.9 0.0 copy-start.1
  2.9 1.6 %copy-done.1 = f32[256,2048]{1,0:T(8,128)S(1)} copy-done((f32[256,2048]{1,0:T(8,128)S(1)}, f32[256,2048]{1,0:T(8,128)}, u32[]{:S(2)}) %copy-start.1) | copy-done | bytes 2097176
  4.5 0.0 copy-start.2
  4.5 1.0 %copy-done.2 = f32[2048,64]{0,1:T(8,128)S(1)} copy-done((f32[2048,64]{0,1:T(8,128)S(1)}, f32[2048,64]{0,1:T(8,128)}, u32[]{:S(2)}) %copy-start.2) | copy-done | bytes 524312
  5.5 0.0 copy-start.5
  5.5 0.7 copy-done.5
  6.2 0.0 copy-start.3
  6.2 0.0 copy-start.4
  6.2 57.3 %exchange.1 = (f32[256,512]{1,0:T(8,128)S(1)}, f32[4,64,768]{2,1,0:T(8,128)S(1)}, f32[128,256]{1,0:T(8,128)S(1)}, bf16[2048,256]{1,0:T(8,128)(2,1)S(1)}, bf16[2048,256]{1,0:T(8,128)(2,1)S(1)}) custom-call(s32[256]{0:T(256)S(1)} %copy-done.5, s32[1,256]{1,0:T(1,128)S(1)} %bitcast.7, f32[64,2048]{1,0:T(8,128)S(1)} %bitcast.6, f32[2048,512]{1,0:T(8,128)S(1)} %copy-done, ...), custom_call_target="tpu_custom_call" | custom-call | tf_op jit(solution)/shard_map/exchange/pallas_call | solution.py:382
  63.5 0.0 copy-done.3
  63.5 0.0 copy-done.4
  63.5 7.5 %update.1 = (f32[2048,512]{1,0:T(8,128)}, f32[64,2048]{1,0:T(8,128)}, f32[64,256]{1,0:T(8,128)}) custom-call(s32[2]{0:T(128)S(1)} %pad_add_fusion.info, s32[1,256]{1,0:T(1,128)S(1)} %bitcast.8, f32[2048,512]{1,0:T(8,128)S(1)} %copy-done, bf16[2048,256]{1,0:T(8,128)(2,1)S(1)} %get-tuple-element.11.ph, bf16[2048,256]{1,0:T(8,128)(2,1)S(1)} %get-tuple-element.12.plo, ...), custom_call_target="tpu_custom_call" | custom-call | tf_op jit(solution)/shard_map/update/pallas_call | solution.py:428
Async XLA Ops:
  0.7 2.2 %copy-start = (f32[2048,512]{1,0:T(8,128)S(1)}, f32[2048,512]{1,0:T(8,128)}, u32[]{:S(2)}) copy-start(f32[2048,512]{1,0:T(8,128)} %look.3) | copy-start | bytes 12582916
  2.9 1.6 %copy-start.1 = (f32[256,2048]{1,0:T(8,128)S(1)}, f32[256,2048]{1,0:T(8,128)}, u32[]{:S(2)}) copy-start(f32[256,2048]{1,0:T(8,128)} %smap.1) | copy-start | bytes 6291460
  4.5 1.0 %copy-start.2 = (f32[2048,64]{0,1:T(8,128)S(1)}, f32[2048,64]{0,1:T(8,128)}, u32[]{:S(2)}) copy-start(f32[2048,64]{0,1:T(8,128)} %param.6) | copy-start | bytes 1572868
  5.5 0.7 copy-start.5
  6.2 57.3 %copy-start.3 = (f32[256,256]{1,0:T(8,128)S(1)}, f32[256,256]{1,0:T(8,128)}, u32[]{:S(2)}) copy-start(f32[256,256]{1,0:T(8,128)} %upper.1) | copy-start | bytes 786436
  6.2 57.3 %copy-start.4 = (f32[256,256]{1,0:T(8,128)S(1)}, f32[256,256]{1,0:T(8,128)}, u32[]{:S(2)}) copy-start(f32[256,256]{1,0:T(8,128)} %lower.1) | copy-start | bytes 786436

commit v2 on v1

--- a/solution.py
+++ b/solution.py
@@ -23,12 +23,13 @@
 S_GZ = 45
 S_GC = 52
 H_X = 53
-H_Z = 56
-H_Y = 63
-H_GZ = 66
-H_GY = 73
-H_GC = 76
-N_SEM = 77
+H_S = 57
+H_R = 89
+H_GZ = 90
+H_GY = 97
+H_GC = 100
+N_SEM = 101
+CHIPS = CY * CZ
 
 
 def split(a):
@@ -46,9 +47,9 @@
 
 
 def comm_kernel(
-    piv_s, piv_v, panel, look, smap,
-    piv, head, red, ph, plo,
-    look_v, sm_v, gath, pick, cbuf, hsum, ybuf, zin, zbuf,
+    pivots, piv_row, panel, look, smap,
+    piv, head, phead, red, ph, plo,
+    piv_s, piv_v, look_v, sm_v, gath, pick, cbuf, hsum, ybuf, zin, zbuf,
     spart, scbuf, ssum, szbuf, sybuf, deal,
     ld, ss, rs,
 ):
@@ -57,7 +58,6 @@
     y = lax.rem(lax.div(r, 2), CY)
     z = lax.div(r, 2 * CY)
     first = r * look.shape[0]
-    root = r == 0
 
     def to_x(d):
         return (r, lax.rem(x + d + 4, 4))
@@ -97,6 +97,12 @@
     halves = [pl.ds(0, half_cols), pl.ds(half_cols, half_cols)]
     own_block = rows64(x)
 
+    load_piv = [
+        pltpu.make_async_copy(pivots, piv_s, ld.at[3]),
+        pltpu.make_async_copy(piv_row, piv_v, ld.at[4]),
+    ]
+    for copy in load_piv:
+        copy.start()
     load_look = pltpu.make_async_copy(look, look_v, ld.at[0])
     load_look.start()
     load_panel = pltpu.make_async_copy(panel, gath.at[own_block, :], ld.at[1])
@@ -105,11 +111,26 @@
     load_map.start()
 
     bar = pltpu.get_barrier_semaphore()
-    partners = [to_x(d) for d in (1, 2, 3)] + [to_y(d) for d in range(1, CY)]
-    partners += [to_z(d) for d in range(1, CZ)] + [sibling]
+    partners = [to_x(1), to_x(3), sibling]
+    partners += [to_y(d) for d in range(1, CY)] + [to_z(d) for d in range(1, CZ)]
+
+    def greet(device):
+        pl.semaphore_signal(bar, inc=1, device_id=device, device_id_type=MESH)
+
     for device in partners:
-        pl.semaphore_signal(bar, inc=1, device_id=device, device_id_type=MESH)
-
+        greet(device)
+
+    @pl.when((y > 0) & (z > 0))
+    def _():
+        greet((c, x))
+
+    @pl.when(r == 1)
+    def _():
+        for d in range(1, 4):
+            greet((0, lax.rem(x + d, 4)))
+
+
+    load_piv[0].wait()
     load_look.wait()
 
     def pick_rows(i, carry):
@@ -122,7 +143,19 @@
         return carry
 
     lax.fori_loop(0, NB // 8, pick_rows, 0)
-    pl.semaphore_wait(bar, len(partners))
+    far = (CY - 1) * (CZ - 1)
+
+    @pl.when(r == 0)
+    def _():
+        pl.semaphore_wait(bar, len(partners) + far + 3)
+
+    @pl.when(r == 1)
+    def _():
+        pl.semaphore_wait(bar, len(partners) + far)
+
+    @pl.when(r > 1)
+    def _():
+        pl.semaphore_wait(bar, len(partners))
 
     a_core = []
     for d in (1, 2, 3, 0):
@@ -137,25 +170,31 @@
         send(panel.at[:, halves[0]], gath.at[own_block, halves[0]], X_RING + 3, left),
     ]
 
-    @pl.when(root)
-    def _():
-        local = [pltpu.make_async_copy(panel.at[:, pl.ds(0, NB)], deal.at[x, :, pl.ds(512, NB)], ld.at[3])]
-        for q in range(CY):
-            local.append(
-                pltpu.make_async_copy(look.at[pl.ds(64 * q, 64), :], deal.at[q, :, pl.ds(0, 512)], ld.at[4 + q])
-            )
-        for copy in local:
-            copy.start()
-        sends = []
-        for d in (1, 2, 3):
-            sends.append(
-                remote(panel.at[:, pl.ds(0, NB)], deal.at[x, :, pl.ds(512, NB)], H_X + d - 1, to_x(d))
-            )
-            sends[-1].start()
-        for copy in local:
-            copy.wait()
-        for copy in sends:
-            copy.wait()
+    def share(ref, q):
+        return ref.at[rows8(lax.rem(q, CY) * CZ + lax.div(q, CY)), :]
+
+    def deal_out(src, dst):
+        def one(q, carry):
+            remote(share(src, q), share(dst, q), H_S + q, (2 * q + c, x), H_R).start()
+            return carry
+
+        lax.fori_loop(1, CHIPS, one, 0)
+
+    def dealt(src, dst):
+        def one(q, carry):
+            remote(share(src, q), share(dst, q), H_S + q, (2 * q + c, x), H_R).wait_send()
+            return carry
+
+        lax.fori_loop(1, CHIPS, one, 0)
+
+    own_head = pltpu.make_async_copy(look.at[pl.ds(0, 8), :], head.at[pl.ds(0, 8), :], ld.at[5])
+
+    @pl.when(r == 0)
+    def _():
+        for to in range(4):
+            remote(panel.at[:, pl.ds(0, NB)], deal.at[rows64(x), :], H_X + to, (1, to), H_X + x).start()
+        own_head.start()
+        deal_out(look, head)
 
     a_y = []
     for d, block, copy in a_core:
@@ -164,12 +203,16 @@
         if d:
             a_y.append(send(hsum.at[block, :], ybuf.at[d - 1], A_Y + d - 1, to_y(d)))
 
-    @pl.when(root)
-    def _():
-        for d in range(1, CZ):
-            remote(deal.at[:, pl.ds(8 * d, 8), :], deal.at[:, pl.ds(8 * d, 8), :], H_Z + d - 1, to_z(d), H_Z).start()
+    @pl.when(r == 1)
+    def _():
+        for q in range(4):
+            block = deal.at[pl.ds(64 * q, 64), :]
+            remote(block, block, H_X + q, sibling).wait_recv()
+        phead[pl.ds(0, 8), :] = deal[pl.ds(0, 8), :]
+        deal_out(deal, phead)
 
     load_panel.wait()
+    load_piv[1].wait()
     load_map.wait()
     spart[...] = jnp.zeros_like(spart)
     tile = 512
@@ -197,31 +240,51 @@
     zin[...] = hsum[rows64(y), :] + ybuf[0] + ybuf[1] + ybuf[2]
     a_z = [send(zin.at[rows8(lax.rem(z + d, CZ)), :], zbuf.at[d - 1], A_Z + d - 1, to_z(d)) for d in range(1, CZ)]
 
-    my_head = head.at[y, rows8(z), :]
-
-    @pl.when((y == 0) & (c == 0))
-    def _():
-        @pl.when(z > 0)
-        def _():
-            landed = deal.at[:, rows8(z), :]
-            remote(landed, landed, H_Z, to_z(1)).wait_recv()
-
-        for d in range(1, CY):
-            remote(deal.at[d, rows8(z), :], head.at[d, rows8(z), :], H_Y + d - 1, to_y(d), H_Y).start()
-        head[0, rows8(z), :] = deal[0, rows8(z), :]
-
     s_core.wait_recv()
     ssum[...] = spart[rows64(c), :] + scbuf[...]
     s_z = [send(ssum.at[rows8(lax.rem(z + d, CZ)), :], szbuf.at[d - 1], S_Z + d - 1, to_z(d)) for d in range(1, CZ)]
 
-    @pl.when(c == 0)
-    def _():
-        @pl.when(y > 0)
+    at_mine = rows8(y * CZ + z)
+    own_rows = rows64(y)
+
+    def by_core(stage):
+        pl.when(c == 0)(lambda: stage(head))
+        pl.when(c == 1)(lambda: stage(phead))
+
+    def head_over_z(buf):
+        own = buf.at[at_mine, :]
+
+        @pl.when(r > 1)
         def _():
-            remote(my_head, my_head, H_Y, to_y(1)).wait_recv()
+            remote(own, own, H_R, sibling).wait_recv()
 
         for d in range(1, CZ):
-            remote(my_head, my_head, H_GZ + d - 1, to_z(d)).start()
+            remote(own, own, H_GZ + d - 1, to_z(d)).start()
+
+    def head_over_y(buf):
+        own = buf.at[at_mine, :]
+        for d in range(1, CZ):
+            remote(own, own, H_GZ + d - 1, to_z(d)).wait_recv()
+        for d in range(1, CY):
+            remote(buf.at[own_rows, :], buf.at[own_rows, :], H_GY + d - 1, to_y(d)).start()
+
+    def head_over_core(buf):
+        own = buf.at[own_rows, :]
+        for d in range(1, CY):
+            remote(own, own, H_GY + d - 1, to_y(d)).wait_recv()
+        remote(buf, buf, H_GC, sibling).start()
+
+    def head_left(buf):
+        own = buf.at[at_mine, :]
+        for d in range(1, CZ):
+            remote(own, own, H_GZ + d - 1, to_z(d)).wait_send()
+        own = buf.at[own_rows, :]
+        for d in range(1, CY):
+            remote(own, own, H_GY + d - 1, to_y(d)).wait_send()
+        remote(buf, buf, H_GC, sibling).wait_send()
+
+    pl.when(r == 0)(own_head.wait)
+    by_core(head_over_z)
 
     ring[0].wait_recv()
     block = gath.at[rows64(lax.rem(x + 3, 4)), halves[0]]
@@ -232,7 +295,6 @@
 
     for copy in a_z:
         copy.wait_recv()
-    at_mine = pl.ds(pl.multiple_of(y * 64 + z * 8, 8), 8)
     total = zin[rows8(z), :]
     for d in range(1, CZ):
         total = total + zbuf[d - 1]
@@ -240,12 +302,7 @@
     chunk = piv.at[at_mine, mine]
     a_gz = [send(chunk, chunk, A_GZ + d - 1, to_z(d)) for d in range(1, CZ)]
 
-    @pl.when(c == 0)
-    def _():
-        for d in range(1, CZ):
-            remote(my_head, my_head, H_GZ + d - 1, to_z(d)).wait_recv()
-        for d in range(1, CY):
-            remote(head.at[y], head.at[y], H_GY + d - 1, to_y(d)).start()
+    by_core(head_over_y)
 
     for copy in s_z:
         copy.wait_recv()
@@ -267,11 +324,7 @@
     red[at_small, :] = sybuf[0] + sybuf[1] + sybuf[2] + sybuf[3]
     s_gz = [send(red.at[at_small, :], red.at[at_small, :], S_GZ + d - 1, to_z(d)) for d in range(1, CZ)]
 
-    @pl.when(c == 0)
-    def _():
-        for d in range(1, CY):
-            remote(head.at[y], head.at[y], H_GY + d - 1, to_y(d)).wait_recv()
-        remote(head, head, H_GC, sibling).start()
+    by_core(head_over_core)
 
     for copy in ring[2:]:
         copy.wait_recv()
@@ -297,35 +350,31 @@
         copy.wait_recv()
     s_gc.wait_recv()
 
+    @pl.when(c == 0)
+    def _():
+        remote(phead, phead, H_GC, sibling).wait_recv()
+
     @pl.when(c == 1)
     def _():
         remote(head, head, H_GC, sibling).wait_recv()
 
     for copy in pending:
         copy.wait_send()
-
-    @pl.when(c == 0)
-    def _():
-        remote(head, head, H_GC, sibling).wait_send()
-        for d in range(1, CZ):
-            remote(my_head, my_head, H_GZ + d - 1, to_z(d)).wait_send()
-        for d in range(1, CY):
-            remote(head.at[y], head.at[y], H_GY + d - 1, to_y(d)).wait_send()
-
-    @pl.when((y == 0) & (c == 0))
-    def _():
-        for d in range(1, CY):
-            remote(deal.at[d, rows8(z), :], head.at[d, rows8(z), :], H_Y + d - 1, to_y(d)).wait_send()
-
-    @pl.when(root)
-    def _():
-        for d in range(1, CZ):
-            part = deal.at[:, pl.ds(8 * d, 8), :]
-            remote(part, part, H_Z + d - 1, to_z(d)).wait_send()
+    by_core(head_left)
+
+    @pl.when(r == 0)
+    def _():
+        for to in range(4):
+            remote(panel.at[:, pl.ds(0, NB)], deal.at[rows64(x), :], H_X + to, (1, to), H_X + x).wait_send()
+        dealt(look, head)
+
+    @pl.when(r == 1)
+    def _():
+        dealt(deal, phead)
 
 
 def update_kernel(
-    info, piv_v, look, ph, plo, piv, head, red, upper, lower,
+    info, piv_v, look, ph, plo, piv, head, phead, red, upper, lower,
     out, lp, sk,
     vh, vl, th, tl, ut, uh, ul, fh, fl, ur,
 ):
@@ -343,9 +392,8 @@
         ur[...] = u_rows
         v = split(dot3(split(up), split(u_rows)))
         vh[...], vl[...] = v
-        rows = head[...].reshape(NB, 768)
-        cols = split(rows[:, 512:])
-        t = rows[:, :512] - dot3(split(rows[:, 512:].T), v)
+        cols = split(phead[...])
+        t = head[...] - dot3(split(phead[...].T), v)
         th[...], tl[...] = split(t)
         ut[...] = up.T
         u = split(ut[pl.ds(pl.multiple_of(x * 64, 64), 64), :])
@@ -378,19 +426,22 @@
     piv_row = pivots.reshape(1, NB)
     vmem = pl.BlockSpec(memory_space=pltpu.VMEM)
     smem = pl.BlockSpec(memory_space=pltpu.SMEM)
-    hbm = pl.BlockSpec(memory_space=pl.ANY)
-    piv, head, red, ph, plo = pl.pallas_call(
+    hbm = pl.BlockSpec(memory_space=pltpu.HBM)
+    piv, head, phead, red, ph, plo = pl.pallas_call(
         comm_kernel,
         out_shape=(
             jax.ShapeDtypeStruct((NB, width), F32),
-            jax.ShapeDtypeStruct((CY, 64, width + NB), F32),
+            jax.ShapeDtypeStruct((NB, width), F32),
+            jax.ShapeDtypeStruct((NB, NB), F32),
             jax.ShapeDtypeStruct((128, NB), F32),
             jax.ShapeDtypeStruct((rows, NB), BF16),
             jax.ShapeDtypeStruct((rows, NB), BF16),
         ),
-        in_specs=[smem, vmem, hbm, hbm, hbm],
-        out_specs=(vmem,) * 5,
+        in_specs=[hbm] * 5,
+        out_specs=(vmem,) * 6,
         scratch_shapes=[
+            pltpu.SMEM((NB,), jnp.int32),
+            pltpu.VMEM((1, NB), jnp.int32),
             pltpu.VMEM((rows, width), F32),
             pltpu.VMEM((NB, rows), F32),
             pltpu.VMEM((NB, rows), F32),
@@ -405,7 +456,7 @@
             pltpu.VMEM((64, NB), F32),
             pltpu.VMEM((7, 8, NB), F32),
             pltpu.VMEM((4, 8, NB), F32),
-            pltpu.VMEM((CY, 64, width + NB), F32),
+            pltpu.VMEM((NB, NB), F32),
             pltpu.SemaphoreType.DMA((8,)),
             pltpu.SemaphoreType.DMA((N_SEM,)),
             pltpu.SemaphoreType.DMA((N_SEM,)),
@@ -414,7 +465,7 @@
             collective_id=0, has_side_effects=True, vmem_limit_bytes=40 << 20
         ),
         name="exchange",
-    )(pivots, piv_row, panel_t, look_cols, sketch_map)
+    )(*[pltpu.with_memory_space_constraint(a, pltpu.HBM) for a in (pivots, piv_row, panel_t, look_cols, sketch_map)])
 
     info = jnp.stack([lax.axis_index("row") * rows, lax.axis_index("col")]).astype(jnp.int32)
     tile = 512
@@ -435,7 +486,7 @@
         ),
         in_specs=[
             smem, whole((1, NB)), by_row(width), by_row(NB), by_row(NB),
-            whole((NB, width)), whole((CY, 64, width + NB)), whole((128, NB)), whole((NB, NB)), whole((NB, NB)),
+            whole((NB, width)), whole((NB, width)), whole((NB, NB)), whole((128, NB)), whole((NB, NB)), whole((NB, NB)),
         ],
         out_specs=(by_row(width), pl.BlockSpec((64, tile), lambda i: (0, i)), whole((64, NB))),
         scratch_shapes=[
@@ -452,7 +503,7 @@
         ],
         compiler_params=pltpu.CompilerParams(vmem_limit_bytes=32 << 20),
         name="update",
-    )(info, piv_row, look_cols, ph, plo, piv, head, red, upper_inv, lower_inv)
+    )(info, piv_row, look_cols, ph, plo, piv, head, phead, red, upper_inv, lower_inv)
     return lp.T, updated, sk.T
 
 

time: 71.3 us -> 56.6 us (0.79)
  the two profiles are of different devices: /device:TPU:1 before, /device:TPU:9 now
where the time goes in v2:
time: 56.6 us
  Pallas kernels  55.8 us (99%)
  between operations  0.71 us (1%)
    pallas_call x1, Pallas kernels, on_device(): pl.pallas_call(comm_kernel, out_shape=(jax.ShapeDtypeStruct((NB, width),...  48.4 us
    pallas_call x1, Pallas kernels, on_device(): pl.pallas_call(update_kernel, grid=(rows // tile,), out_shape=(jax.ShapeD...  7.36 us

profile of v2, /device:TPU:9, one launch (start us, length us, event | category | flops | bytes accessed | tf_op | source)
XLA Modules:
  0.0 56.6 jit_solution(9521634501286326114)
XLA Ops:
  0.6 0.0 copy-start.3
  0.6 0.0 copy-start.2
  0.7 0.0 copy-start.1
  0.7 0.0 copy-start
  0.7 0.1 pad_add_fusion.info
  0.8 48.4 %exchange.1 = (f32[256,512]{1,0:T(8,128)S(1)}, f32[256,512]{1,0:T(8,128)S(1)}, f32[256,256]{1,0:T(8,128)S(1)}, f32[128,256]{1,0:T(8,128)S(1)}, bf16[2048,256]{1,...) custom-call(s32[256]{0:T(256)} %pivots.1, s32[1,256]{1,0:T(1,128)} %bitcast.6, f32[64,2048]{1,0:T(8,128)} %bitcast.8, ...), custom_call_target="tpu_custom_call" | custom-call | tf_op jit(solution)/shard_map/exchange/pallas_call | solution.py:430
  49.2 0.0 copy-done.3
  49.2 0.0 copy-done.2
  49.2 0.0 copy-done.1
  49.2 0.0 copy-done
  49.2 7.4 %update.1 = (f32[2048,512]{1,0:T(8,128)}, f32[64,2048]{1,0:T(8,128)}, f32[64,256]{1,0:T(8,128)}) custom-call(s32[2]{0:T(128)S(1)} %pad_add_fusion.info, s32[1,256]{1,0:T(1,128)S(1)} %bitcast.7, f32[2048,512]{1,0:T(8,128)S(1)} %copy-done, bf16[2048,256]{1,0:T(8,128)(2,1)S(1)} %get-tuple-element.12.ph, bf16[2048,256]{1,0:T(8,128)(2,1)S(1)} %get-tuple-element.13.plo, ...), custom_call_target="tpu_custom_call" | custom-call | tf_op jit(solution)/shard_map/update/pallas_call | solution.py:479
Async XLA Ops:
  0.6 48.5 %copy-start.3 = (s32[256]{0:T(256)S(1)}, s32[256]{0:T(256)}, u32[]{:S(2)}) copy-start(s32[256]{0:T(256)} %pivots.1) | copy-start | bytes 3076
  0.6 48.5 %copy-start.2 = (f32[256,256]{1,0:T(8,128)S(1)}, f32[256,256]{1,0:T(8,128)}, u32[]{:S(2)}) copy-start(f32[256,256]{1,0:T(8,128)} %lower.1) | copy-start | bytes 786436
  0.7 48.5 %copy-start.1 = (f32[256,256]{1,0:T(8,128)S(1)}, f32[256,256]{1,0:T(8,128)}, u32[]{:S(2)}) copy-start(f32[256,256]{1,0:T(8,128)} %upper.1) | copy-start | bytes 786436
  0.7 48.5 %copy-start = (f32[2048,512]{1,0:T(8,128)S(1)}, f32[2048,512]{1,0:T(8,128)}, u32[]{:S(2)}) copy-start(f32[2048,512]{1,0:T(8,128)} %look.3) | copy-start | bytes 12582916

commit v3 on v0

v3 whole, which is shorter than its diff:
```python
import jax
import jax.numpy as jnp
from jax import lax
from jax.experimental import pallas as pl
from jax.experimental.pallas import tpu as pltpu
from jax.sharding import PartitionSpec as P

MESH = pl.DeviceIdType.MESH
F32, BF16 = jnp.float32, jnp.bfloat16
NB = 256
CY, CZ = 4, 8
CHIPS = CY * CZ

X_RING = 0
A_CORE = 6
A_Y = 10
A_Z = 14
A_GZ = 22
A_GY = 42
A_GC = 74
S_CORE = 78
S_Y = 79
S_Z = 83
S_GY = 91
S_GC = 95
H_X = 96
H_S = 100
H_R = 132
H_GZ = 133
H_GY = 141
H_GC = 173
N_SEM = 177

FAR_Z = (4, 3, 5, 2, 6, 1, 7)
NEAR_Z = (1, 7, 2, 6, 3, 5, 4)


def split(a):
    hi = a.astype(BF16)
    return hi, (a - hi.astype(F32)).astype(BF16)


def dot(a, b, dims=((1,), (0,))):
    return lax.dot_general(a, b, (dims, ((), ())), preferred_element_type=F32)


def dot3(a, b):
    (ah, al), (bh, bl) = a, b
    return dot(ah, bh) + dot(al, bh) + dot(ah, bl)


def exchange_kernel(
    pivots, piv_row, panel, look, smap, upper, lower,
    left_ref, va, vb, ur, lp, sk,
    piv_s, piv_v, look_v, sm_v, up_v, low_v, gath, hot_t, hit,
    pick, cbuf, hsum, ybuf, zin, zbuf, piv, head, phead, deal,
    spart, scbuf, ssum, sybuf, szbuf, red,
    ld, ss, rs,
):
    r, x = lax.axis_index("row"), lax.axis_index("col")
    c = lax.rem(r, 2)
    y = lax.rem(lax.div(r, 2), CY)
    z = lax.div(r, 2 * CY)
    rows = look.shape[0]
    first = r * rows

    def chip(dy, dz):
        return ((lax.rem(z + dz, CZ) * CY + lax.rem(y + dy, CY)) * 2 + c, x)

    def to_x(d):
        return (r, lax.rem(x + d + 4, 4))

    sibling = ((z * CY + y) * 2 + 1 - c, x)
    pending = []

    def remote(src, dst, slot, device, recv_slot=None):
        return pltpu.make_async_remote_copy(
            src_ref=src, dst_ref=dst, send_sem=ss.at[slot],
            recv_sem=rs.at[slot if recv_slot is None else recv_slot],
            device_id=device, device_id_type=MESH,
        )

    def send(*args):
        copy = remote(*args)
        copy.start()
        pending.append(copy)
        return copy

    def block_of(i, n):
        return pl.ds(pl.multiple_of(i * n, n), n)

    def rows_of(dy, dz):
        return block_of(lax.rem(y + dy, CY) * CZ + lax.rem(z + dz, CZ), 8)

    mine, other = block_of(c, 256), block_of(1 - c, 256)
    half_cols = rows // 2
    halves = [pl.ds(0, half_cols), pl.ds(half_cols, half_cols)]
    own_block = block_of(x, 64)

    loads = {}
    for i, (name, src, dst) in enumerate(
        (
            ("piv_s", pivots, piv_s),
            ("look", look, look_v),
            ("piv_v", piv_row, piv_v),
            ("panel", panel, gath.at[own_block, :]),
            ("map", smap, sm_v),
            ("upper", upper, up_v),
            ("lower", lower, low_v),
        )
    ):
        loads[name] = pltpu.make_async_copy(src, dst, ld.at[i])
        loads[name].start()

    bar = pltpu.get_barrier_semaphore()

    def greet(device):
        pl.semaphore_signal(bar, inc=1, device_id=device, device_id_type=MESH)

    partners = [chip(d, 0) for d in range(1, CY)] + [chip(0, d) for d in range(1, CZ)]
    partners += [to_x(1), to_x(3), sibling]
    for device in partners:
        greet(device)

    @pl.when((y > 0) & (z > 0))
    def _():
        greet((c, x))

    @pl.when(r == 1)
    def _():
        for d in range(1, 4):
            greet((0, lax.rem(x + d, 4)))

    loads["piv_s"].wait()
    loads["look"].wait()

    def pick_rows(i, carry):
        for k in range(8):
            row = i * 8 + k
            local = piv_s[row] - first
            owned = (local >= 0) & (local < rows)
            at = jnp.where(owned, local, 0)
            pick[pl.ds(row, 1), :] = jnp.where(owned, look_v[pl.ds(at, 1), :], 0.0)
        return carry

    lax.fori_loop(0, NB // 8, pick_rows, 0)

    far = (CY - 1) * (CZ - 1)

    @pl.when(r == 0)
    def _():
        pl.semaphore_wait(bar, len(partners) + far + 3)

    @pl.when(r == 1)
    def _():
        pl.semaphore_wait(bar, len(partners) + far)

    @pl.when(r > 1)
    def _():
        pl.semaphore_wait(bar, len(partners))

    a_core = []
    for d in (2, 1, 3, 0):
        block = block_of(lax.rem(y + d, CY), 64)
        a_core.append((d, block, send(pick.at[block, other], cbuf.at[block, :], A_CORE + d, sibling)))

    def share(ref, q):
        return ref.at[block_of(lax.rem(q, CY) * CZ + lax.div(q, CY), 8), :]

    def shares(src, dst, act):
        def one(q, carry):
            act(remote(share(src, q), share(dst, q), H_S + q, (2 * q + c, x), H_R))
            return carry

        lax.fori_loop(1, CHIPS, one, 0)

    def columns(to):
        return remote(panel.at[:, pl.ds(0, NB)], deal.at[own_block, :], H_X + to, (1, to), H_X + x)

    own_head = pltpu.make_async_copy(look.at[pl.ds(0, 8), :], head.at[pl.ds(0, 8), :], ld.at[7])

    @pl.when(r == 0)
    def _():
        for to in range(4):
            columns(to).start()
        own_head.start()
        shares(look, head, lambda copy: copy.start())

    right, left = to_x(1), to_x(3)
    ring = [
        send(panel.at[:, halves[0]], gath.at[own_block, halves[0]], X_RING, right),
        send(panel.at[:, halves[1]], gath.at[own_block, halves[1]], X_RING + 2, left),
        send(panel.at[:, halves[1]], gath.at[own_block, halves[1]], X_RING + 1, right),
        send(panel.at[:, halves[0]], gath.at[own_block, halves[0]], X_RING + 3, left),
    ]

    a_y = []
    for d, block, copy in a_core:
        copy.wait_recv()
        hsum[block, :] = pick[block, mine] + cbuf[block, :]
        if d:
            a_y.append(send(hsum.at[block, :], ybuf.at[d - 1], A_Y + d, chip(d, 0)))

    @pl.when(r == 1)
    def _():
        for q in range(4):
            block = deal.at[pl.ds(64 * q, 64), :]
            remote(block, block, H_X + q, sibling).wait_recv()
        phead[pl.ds(0, 8), :] = deal[pl.ds(0, 8), :]
        shares(deal, phead, lambda copy: copy.start())

    loads["panel"].wait()
    loads["piv_v"].wait()
    loads["map"].wait()
    spart[...] = jnp.zeros_like(spart)
    tile = 256
    wide = jnp.broadcast_to(piv_v[...], (NB, NB))
    tall = wide.T

    def small(i, carry):
        cols = block_of(i, tile)
        p = gath[own_block, cols]
        p1, p2 = split(p)
        p3 = (p - p1.astype(F32) - p2.astype(F32)).astype(BF16)
        mh, ml = split(sm_v[:, cols])
        nt = ((1,), (1,))
        both = dot(jnp.concatenate([p1, p2], 0), mh, nt)
        spart[0:64, :] += both[0:64] + both[64:128] + dot(p1, ml, nt)
        start = first + i * tile
        at = lax.broadcasted_iota(jnp.int32, (tile, NB), 0) + start
        hot = jnp.where(at == wide, 1.0, 0.0).astype(BF16)
        left_ref[cols, 512:768] = hot
        at = lax.broadcasted_iota(jnp.int32, (NB, tile), 1) + start
        turned = jnp.where(at == tall, 1.0, 0.0)
        hot_t[:, cols] = turned.astype(BF16)
        hit[:, cols] = jnp.broadcast_to(jnp.max(turned, axis=0, keepdims=True), (8, tile))
        three = dot(jnp.concatenate([p1, p2, p3], 0), hot)
        spart[64:128, :] += three[0:64] + three[64:128] + three[128:192]
        return carry

    lax.fori_loop(0, rows // tile, small, 0)
    s_core = send(spart.at[block_of(1 - c, 64), :], scbuf, S_CORE, sibling)
    s_core.wait_recv()
    ssum[...] = spart[block_of(c, 64), :] + scbuf[...]
    s_y = [send(ssum.at[block_of(lax.rem(y + d, CY), 16), :], sybuf.at[d - 1], S_Y + d, chip(d, 0)) for d in range(1, CY)]

    for copy in a_y:
        copy.wait_recv()
    zin[...] = hsum[block_of(y, 64), :] + ybuf[0] + ybuf[1] + ybuf[2]
    a_z = [send(zin.at[block_of(lax.rem(z + d, CZ), 8), :], zbuf.at[d - 1], A_Z + d, chip(0, d)) for d in FAR_Z]

    own = rows_of(0, 0)

    def by_core(stage):
        pl.when(c == 0)(lambda: stage(head))
        pl.when(c == 1)(lambda: stage(phead))

    def over_z(buf, d):
        return remote(buf.at[own, :], buf.at[own, :], H_GZ + d, chip(0, d))

    def over_y(buf, d, e):
        part = buf.at[rows_of(0, CZ - e), :]
        return remote(part, part, H_GY + d * CZ + e, chip(d, 0))

    def over_core(buf, d):
        part = buf.at[block_of(lax.rem(y + d, CY), 64), :]
        return remote(part, part, H_GC + d, sibling)

    def head_over_z(buf):
        @pl.when(r > 1)
        def _():
            remote(buf.at[own, :], buf.at[own, :], H_R, sibling).wait_recv()

        for d in FAR_Z:
            over_z(buf, d).start()
        for d in range(1, CY):
            over_y(buf, d, 0).start()

    def head_over_y(buf):
        for e in NEAR_Z:
            over_z(buf, e).wait_recv()
            for d in (2, 1, 3):
                over_y(buf, d, e).start()
        over_core(buf, 0).start()

    def head_over_core(buf):
        for d in (1, 3, 2):
            for e in range(CZ):
                over_y(buf, CY - d, e).wait_recv()
            over_core(buf, d).start()

    def head_arrived(buf):
        for d in range(CY):
            over_core(buf, d).wait_recv()

    def head_left(buf):
        for d in range(1, CZ):
            over_z(buf, d).wait_send()
        for d in range(1, CY):
            for e in range(CZ):
                over_y(buf, d, e).wait_send()
        for d in range(CY):
            over_core(buf, d).wait_send()

    pl.when(r == 0)(own_head.wait)
    by_core(head_over_z)

    for copy in s_y:
        copy.wait_recv()
    szbuf[z] = ssum[block_of(y, 16), :] + sybuf[0] + sybuf[1] + sybuf[2]
    s_z = [send(szbuf.at[z], szbuf.at[z], S_Z + d, chip(0, d)) for d in FAR_Z]

    ring[0].wait_recv()
    block = gath.at[block_of(lax.rem(x + 3, 4), 64), halves[0]]
    ring.append(send(block, block, X_RING + 4, right))
    ring[1].wait_recv()
    block = gath.at[block_of(lax.rem(x + 1, 4), 64), halves[1]]
    ring.append(send(block, block, X_RING + 5, left))

    for copy in a_z:
        copy.wait_recv()
    total = zin[block_of(z, 8), :]
    for d in range(1, CZ):
        total = total + zbuf[d - 1]
    piv[own, mine] = total
    a_gz = {d: send(piv.at[own, mine], piv.at[own, mine], A_GZ + d, chip(0, d)) for d in FAR_Z}
    a_gy = {}

    def a_over_y(e):
        part = piv.at[rows_of(0, CZ - e), mine]
        for d in (2, 1, 3):
            a_gy[d, e] = send(part, part, A_GY + d * CZ + e, chip(d, 0))

    a_over_y(0)
    by_core(head_over_y)
    for e in NEAR_Z:
        a_gz[e].wait_recv()
        a_over_y(e)
    a_gc = []
    for d in (0, 1, 3, 2):
        for e in range(CZ):
            if d:
                a_gy[CY - d, e].wait_recv()
        part = piv.at[block_of(lax.rem(y + d, CY), 64), mine]
        a_gc.append(send(part, part, A_GC + d, sibling))

    for copy in s_z:
        copy.wait_recv()
    total = szbuf[0]
    for q in range(1, CZ):
        total = total + szbuf[q]
    at_small = block_of(c * CY + y, 16)
    red[at_small, :] = total
    s_gy = [send(red.at[at_small, :], red.at[at_small, :], S_GY + d, chip(d, 0)) for d in range(1, CY)]

    loads["upper"].wait()
    loads["lower"].wait()
    i = lax.broadcasted_iota(jnp.int32, (NB, NB), 0)
    j = lax.broadcasted_iota(jnp.int32, (NB, NB), 1)
    low = split(jnp.where(i > j, low_v[...], jnp.where(i == j, 1.0, 0.0)))
    up = jnp.where(i <= j, up_v[...], 0.0)
    low_v[...] = up.T
    u = split(low_v[own_block, :])
    both_u = jnp.concatenate(u, 0)
    for copy in a_gc:
        copy.wait_recv()
    u_rows = dot3(low, split(piv[...]))
    ur[...] = u_rows
    vh, vl = split(dot3(split(up), split(u_rows)))
    va[0:256, :] = -vh
    va[256:512, :] = -vh
    vb[0:256, :] = -vl

    by_core(head_over_core)

    for copy in ring[2:]:
        copy.wait_recv()

    def turn(i, carry):
        at = block_of(i, 256)
        kept = jnp.where(hit[0:1, at] > 0.0, 0.0, gath[:, at])
        hi, lo = split(kept)
        pre = dot(both_u, hi)
        lp[:, at] = pre[0:64] + pre[64:128] + dot(u[0], lo)
        hi, lo = split(kept.T)
        left_ref[at, 0:256] = lo
        left_ref[at, 256:512] = hi
        return carry

    lax.fori_loop(0, rows // 256, turn, 0)

    for copy in s_gy:
        copy.wait_recv()
    part = red.at[block_of(c, 64), :]
    s_gc = send(part, part, S_GC, sibling)

    pl.when(c == 0)(lambda: head_arrived(phead))
    pl.when(c == 1)(lambda: head_arrived(head))
    moved = (head[...] - piv[...]) - dot3(split(phead[...].T), (vh, vl))
    dh, dl = split(moved)
    va[512:768, :] = dh
    vb[256:512, :] = dl
    both_f = jnp.concatenate(split(dot3(u, split(phead[...]))), 0)

    def moved_factor(i, carry):
        at = block_of(i, 256)
        add = dot(both_f, hot_t[:, at])
        lp[:, at] += add[0:64] + add[64:128]
        return carry

    lax.fori_loop(0, rows // 256, moved_factor, 0)
    s_gc.wait_recv()
    sk[...] = red[0:64, :]

    @pl.when(r == 0)
    def _():
        lp[:, 0:NB] = red[64:128, :]

    for copy in pending:
        copy.wait_send()
    by_core(head_left)

    @pl.when(r == 0)
    def _():
        for to in range(4):
            columns(to).wait_send()
        shares(look, head, lambda copy: copy.wait_send())

    @pl.when(r == 1)
    def _():
        shares(deal, phead, lambda copy: copy.wait_send())


def update_kernel(first, look, left_ref, va, vb, ur, lp, sk, out, lp_out, sk_out, buf, sem, small_sem):
    tile = buf.shape[1]
    steps = buf.shape[0]
    small = [
        pltpu.make_async_copy(lp, lp_out, small_sem.at[0]),
        pltpu.make_async_copy(sk, sk_out, small_sem.at[1]),
    ]
    for copy in small:
        copy.start()

    def block(i):
        return pl.ds(pl.multiple_of(i * tile, tile), tile)

    def write(i):
        return pltpu.make_async_copy(buf.at[i], out.at[block(i), :], sem.at[i])

    def step(i, carry):
        at = block(i)
        buf[i] = look[at, :] + dot(left_ref[at, :], va[...]) + dot(left_ref[at, 256:768], vb[...])

        @pl.when((i == 0) & (first[0] == 0))
        def _():
            buf[0, 0:NB, :] = ur[...]

        write(i).start()
        return carry

    lax.fori_loop(0, steps, step, 0)
    for copy in small:
        copy.wait()
    for i in range(steps):
        write(i).wait()


def on_device(panel_col, look_cols, sketch_map, upper_inv, lower_inv, pivots):
    rows, width = look_cols.shape
    panel_t = panel_col.T
    piv_row = pivots.reshape(1, NB)
    vmem = pl.BlockSpec(memory_space=pltpu.VMEM)
    hbm = pl.BlockSpec(memory_space=pltpu.HBM)
    inputs = [
        pltpu.with_memory_space_constraint(a, pltpu.HBM)
        for a in (pivots, piv_row, panel_t, look_cols, sketch_map, upper_inv, lower_inv)
    ]
    results = pl.pallas_call(
        exchange_kernel,
        out_shape=(
            jax.ShapeDtypeStruct((rows, 3 * NB), BF16),
            jax.ShapeDtypeStruct((3 * NB, width), BF16),
            jax.ShapeDtypeStruct((2 * NB, width), BF16),
            jax.ShapeDtypeStruct((NB, width), F32),
            jax.ShapeDtypeStruct((64, rows), F32),
            jax.ShapeDtypeStruct((64, NB), F32),
        ),
        in_specs=[hbm] * len(inputs),
        out_specs=(vmem,) * 6,
        scratch_shapes=[
            pltpu.SMEM((NB,), jnp.int32),
            pltpu.VMEM((1, NB), jnp.int32),
            pltpu.VMEM((rows, width), F32),
            pltpu.VMEM((NB, rows), F32),
            pltpu.VMEM((NB, NB), F32),
            pltpu.VMEM((NB, NB), F32),
            pltpu.VMEM((NB, rows), F32),
            pltpu.VMEM((NB, rows), BF16),
            pltpu.VMEM((8, rows), F32),
            pltpu.VMEM((NB, width), F32),
            pltpu.VMEM((NB, 256), F32),
            pltpu.VMEM((NB, 256), F32),
            pltpu.VMEM((3, 64, 256), F32),
            pltpu.VMEM((64, 256), F32),
            pltpu.VMEM((7, 8, 256), F32),
            pltpu.VMEM((NB, width), F32),
            pltpu.VMEM((NB, width), F32),
            pltpu.VMEM((NB, NB), F32),
            pltpu.VMEM((NB, NB), F32),
            pltpu.VMEM((128, NB), F32),
            pltpu.VMEM((64, NB), F32),
            pltpu.VMEM((64, NB), F32),
            pltpu.VMEM((3, 16, NB), F32),
            pltpu.VMEM((CZ, 16, NB), F32),
            pltpu.VMEM((128, NB), F32),
            pltpu.SemaphoreType.DMA((8,)),
            pltpu.SemaphoreType.DMA((N_SEM,)),
            pltpu.SemaphoreType.DMA((N_SEM,)),
        ],
        compiler_params=pltpu.CompilerParams(
            collective_id=0, has_side_effects=True, vmem_limit_bytes=36 << 20
        ),
        name="exchange",
    )(*inputs)

    first = (lax.axis_index("row") * rows).astype(jnp.int32).reshape(1)
    tile = 256
    updated, lp, sk = pl.pallas_call(
        update_kernel,
        out_shape=(
            jax.ShapeDtypeStruct((rows, width), F32),
            jax.ShapeDtypeStruct((64, rows), F32),
            jax.ShapeDtypeStruct((64, NB), F32),
        ),
        in_specs=[pl.BlockSpec(memory_space=pltpu.SMEM)] + [vmem] * 7,
        out_specs=(hbm,) * 3,
        scratch_shapes=[
            pltpu.VMEM((rows // tile, tile, width), F32),
            pltpu.SemaphoreType.DMA((rows // tile,)),
            pltpu.SemaphoreType.DMA((2,)),
        ],
        compiler_params=pltpu.CompilerParams(vmem_limit_bytes=32 << 20),
        name="update",
    )(first, look_cols, *results)
    return lp.T, updated, sk.T


def solution(mesh):
    placed = (P("row", "col"), P("row", "col"), P(None, "row"), P(), P(), P())
    return jax.shard_map(
        on_device,
        mesh=mesh,
        in_specs=placed,
        out_specs=(P("row", "col"), P("row", "col"), P(None, "col")),
        check_vma=False,
    )
```

time: 308 us -> 49.3 us (0.16)
  waiting for transfers between devices: 244 us -> 0 us
  Pallas kernels: 0 us -> 48.5 us
  local copies, waits for them, and re-layouts: 22.1 us -> 0.01 us
  matrix products: 18.8 us -> 0 us
  between operations: 14.2 us -> 0.66 us
  other arithmetic: 8.61 us -> 0 us
    psum x2 -> x0, waiting for transfers between devices: 244 us -> none  [the longest x1 190 us: on_device(): lax.psum((sketch_part, panel_pick, look_pick, panel_head, look_head), 'row')]
    pallas_call x0 -> x2, Pallas kernels: none -> 48.5 us  [the longest x1 43.6 us: on_device(): pl.pallas_call(exchange_kernel, out_shape=(jax.ShapeDtypeStruct((rows, 3...]
    dot_general x4 -> x0, matrix products: 18.8 us -> none  [the longest x1 8.65 us: on_device(): jnp.dot(factor, u_rows, precision=high_prec, preferred_element_type=jnp.f...]
    unnamed x16 -> x2, local copies, waits for them, and re-layouts: 9.15 us -> 0.01 us
    select_n x7 -> x0, other arithmetic: 8.48 us -> none  [the longest x1 2.25 us: on_device(): look_head = jnp.where(on_root, look_cols[:block_size], 0.0)]
    scatter x2 -> x0, local copies, waits for them, and re-layouts: 8.03 us -> none  [the longest x1 6.12 us: on_device(): swapped_look = look_cols.at[target].set(look_orig, mode='drop')]
    gather x2 -> x0, local copies, waits for them, and re-layouts: 4.91 us -> none  [the longest x1 4.18 us: on_device(): look_pick = jnp.where(owned_mask, look_cols[local_idx], 0.0)]
  transfers between devices with their start and end apart: 2 -> 0, of which waited for: 2 -> 0; matrix products, arithmetic and copies ran while one was open for 3% -> 0% of each run, Pallas kernels for 0% -> 0%
where the time goes in v3:
time: 49.3 us; the launch traced here: 49.2 us
  Pallas kernels  48.5 us (98%)
  between operations  0.66 us (1%)
    pallas_call x1, Pallas kernels, on_device(): pl.pallas_call(exchange_kernel, out_shape=(jax.ShapeDtypeStruct((rows, 3...  43.6 us
    pallas_call x1, Pallas kernels, on_device(): pl.pallas_call(update_kernel, out_shape=(jax.ShapeDtypeStruct((rows, widt...  4.93 us

profile of v3, /device:TPU:1, one launch (start us, length us, event | category | flops | bytes accessed | tf_op | source)
XLA Modules:
  0.0 49.2 jit_solution(2079702807171393746)
XLA Ops:
  0.6 0.0 copy-start
  0.6 43.6 %exchange.1 = (bf16[2048,768]{1,0:T(8,128)(2,1)S(1)}, bf16[768,512]{1,0:T(8,128)(2,1)S(1)}, bf16[512,512]{1,0:T(8,128)(2,1)S(1)}, f32[256,512]{1,0:T(8,128)S(1)}...) custom-call(s32[256]{0:T(256)} %pivots.1, s32[1,256]{1,0:T(1,128)} %bitcast.6, f32[64,2048]{1,0:T(8,128)} %bitcast.5, ...), custom_call_target="tpu_custom_call" | custom-call | tf_op jit(solution)/shard_map/exchange/pallas_call | solution.py:478
  44.2 0.0 copy-done
  44.2 4.9 %update.1 = (f32[2048,512]{1,0:T(8,128)}, f32[64,2048]{1,0:T(8,128)}, f32[64,256]{1,0:T(8,128)}) custom-call(s32[1]{0:T(128)} %bitcast.first, f32[2048,512]{1,0:T(8,128)S(1)} %copy-done, bf16[2048,768]{1,0:T(8,128)(2,1)S(1)} %get-tuple-element.12.left_ref, bf16[768,512]{1,0:T(8,128)(2,1)S(1)} %get-tuple-element.13.va, ...), custom_call_target="tpu_custom_call" | custom-call | tf_op jit(solution)/shard_map/update/pallas_call | solution.py:528
Async XLA Ops:
  0.6 43.6 %copy-start = (f32[2048,512]{1,0:T(8,128)S(1)}, f32[2048,512]{1,0:T(8,128)}, u32[]{:S(2)}) copy-start(f32[2048,512]{1,0:T(8,128)} %look.3) | copy-start | bytes 12582916

commit v4 on v3

--- a/solution.py
+++ b/solution.py
@@ -14,8 +14,8 @@
 X_RING = 0
 A_CORE = 6
 A_Y = 10
-A_Z = 14
-A_GZ = 22
+A_Z = 18
+A_GZ = 26
 A_GY = 42
 A_GC = 74
 S_CORE = 78
@@ -54,7 +54,7 @@
     left_ref, va, vb, ur, lp, sk,
     piv_s, piv_v, look_v, sm_v, up_v, low_v, gath, hot_t, hit,
     pick, cbuf, hsum, ybuf, zin, zbuf, piv, head, phead, deal,
-    spart, scbuf, ssum, sybuf, szbuf, red,
+    spart, scbuf, ssum, sybuf, szbuf, red, lowh, lowl, mulh, mull, both_u,
     ld, ss, rs,
 ):
     r, x = lax.axis_index("row"), lax.axis_index("col")
@@ -95,7 +95,6 @@
     mine, other = block_of(c, 256), block_of(1 - c, 256)
     half_cols = rows // 2
     halves = [pl.ds(0, half_cols), pl.ds(half_cols, half_cols)]
-    own_block = block_of(x, 64)
 
     loads = {}
     for i, (name, src, dst) in enumerate(
@@ -103,7 +102,7 @@
             ("piv_s", pivots, piv_s),
             ("look", look, look_v),
             ("piv_v", piv_row, piv_v),
-            ("panel", panel, gath.at[own_block, :]),
+            ("panel", panel, gath.at[pl.ds(0, 64), :]),
             ("map", smap, sm_v),
             ("upper", upper, up_v),
             ("lower", lower, low_v),
@@ -135,9 +134,13 @@
     loads["look"].wait()
 
     def pick_rows(i, carry):
+        pos = lax.rem(i, CZ)
+        step = lax.div(pos + 1, 2)
+        dz = jnp.where(lax.rem(pos, 2) == 1, 4 - step, 4 + step)
+        start = (lax.div(i, CZ) * CZ + lax.rem(z + dz, CZ)) * 8
         for k in range(8):
             row = i * 8 + k
-            local = piv_s[row] - first
+            local = piv_s[start + k] - first
             owned = (local >= 0) & (local < rows)
             at = jnp.where(owned, local, 0)
             pick[pl.ds(row, 1), :] = jnp.where(owned, look_v[pl.ds(at, 1), :], 0.0)
@@ -145,15 +148,15 @@
 
     lax.fori_loop(0, NB // 8, pick_rows, 0)
 
-    far = (CY - 1) * (CZ - 1)
+    extra = (CY - 1) * (CZ - 1)
 
     @pl.when(r == 0)
     def _():
-        pl.semaphore_wait(bar, len(partners) + far + 3)
+        pl.semaphore_wait(bar, len(partners) + extra + 3)
 
     @pl.when(r == 1)
     def _():
-        pl.semaphore_wait(bar, len(partners) + far)
+        pl.semaphore_wait(bar, len(partners) + extra)
 
     @pl.when(r > 1)
     def _():
@@ -175,7 +178,7 @@
         lax.fori_loop(1, CHIPS, one, 0)
 
     def columns(to):
-        return remote(panel.at[:, pl.ds(0, NB)], deal.at[own_block, :], H_X + to, (1, to), H_X + x)
+        return remote(panel.at[:, pl.ds(0, NB)], deal.at[block_of(x, 64), :], H_X + to, (1, to), H_X + x)
 
     own_head = pltpu.make_async_copy(look.at[pl.ds(0, 8), :], head.at[pl.ds(0, 8), :], ld.at[7])
 
@@ -188,18 +191,25 @@
 
     right, left = to_x(1), to_x(3)
     ring = [
-        send(panel.at[:, halves[0]], gath.at[own_block, halves[0]], X_RING, right),
-        send(panel.at[:, halves[1]], gath.at[own_block, halves[1]], X_RING + 2, left),
-        send(panel.at[:, halves[1]], gath.at[own_block, halves[1]], X_RING + 1, right),
-        send(panel.at[:, halves[0]], gath.at[own_block, halves[0]], X_RING + 3, left),
+        send(panel.at[:, halves[0]], gath.at[pl.ds(128, 64), halves[0]], X_RING, right),
+        send(panel.at[:, halves[1]], gath.at[pl.ds(64, 64), halves[1]], X_RING + 2, left),
+        send(panel.at[:, halves[1]], gath.at[pl.ds(128, 64), halves[1]], X_RING + 1, right),
+        send(panel.at[:, halves[0]], gath.at[pl.ds(64, 64), halves[0]], X_RING + 3, left),
     ]
 
-    a_y = []
+    def group(block, g):
+        return hsum.at[pl.ds(pl.multiple_of(block * 64 + g * 32, 32), 32), :]
+
+    a_y = {}
     for d, block, copy in a_core:
         copy.wait_recv()
         hsum[block, :] = pick[block, mine] + cbuf[block, :]
         if d:
-            a_y.append(send(hsum.at[block, :], ybuf.at[d - 1], A_Y + d, chip(d, 0)))
+            part = group(lax.rem(y + d, CY), 0)
+            a_y[d, 0] = send(part, ybuf.at[d - 1, pl.ds(0, 32), :], A_Y + d, chip(d, 0))
+    for d in (2, 1, 3):
+        part = group(lax.rem(y + d, CY), 1)
+        a_y[d, 1] = send(part, ybuf.at[d - 1, pl.ds(32, 32), :], A_Y + 4 + d, chip(d, 0))
 
     @pl.when(r == 1)
     def _():
@@ -219,7 +229,7 @@
 
     def small(i, carry):
         cols = block_of(i, tile)
-        p = gath[own_block, cols]
+        p = gath[0:64, cols]
         p1, p2 = split(p)
         p3 = (p - p1.astype(F32) - p2.astype(F32)).astype(BF16)
         mh, ml = split(sm_v[:, cols])
@@ -238,16 +248,41 @@
         spart[64:128, :] += three[0:64] + three[64:128] + three[128:192]
         return carry
 
-    lax.fori_loop(0, rows // tile, small, 0)
+    lax.fori_loop(0, rows // tile, small, 0, unroll=8)
     s_core = send(spart.at[block_of(1 - c, 64), :], scbuf, S_CORE, sibling)
+
+    order = [block_of(lax.rem(x + d, 4), 64) for d in (0, 1, 3, 2)]
+
+    def reorder(ref):
+        return jnp.concatenate([ref[block, :] for block in order], 0)
+
+    loads["upper"].wait()
+    loads["lower"].wait()
+    i = lax.broadcasted_iota(jnp.int32, (NB, NB), 0)
+    j = lax.broadcasted_iota(jnp.int32, (NB, NB), 1)
+    low = split(jnp.where(i > j, low_v[...], jnp.where(i == j, 1.0, 0.0)))
+    up_v[...] = jnp.where(i <= j, up_v[...], 0.0)
+    up = reorder(up_v)
+    lowh[...], lowl[...] = low
+    mulh[...], mull[...] = split(dot3(split(up), low))
+    up_v[...] = up.T
+    u = split(up_v[block_of(x, 64), :])
+    both_u[...] = jnp.concatenate(u, 0)
+
     s_core.wait_recv()
     ssum[...] = spart[block_of(c, 64), :] + scbuf[...]
     s_y = [send(ssum.at[block_of(lax.rem(y + d, CY), 16), :], sybuf.at[d - 1], S_Y + d, chip(d, 0)) for d in range(1, CY)]
 
-    for copy in a_y:
-        copy.wait_recv()
-    zin[...] = hsum[block_of(y, 64), :] + ybuf[0] + ybuf[1] + ybuf[2]
-    a_z = [send(zin.at[block_of(lax.rem(z + d, CZ), 8), :], zbuf.at[d - 1], A_Z + d, chip(0, d)) for d in FAR_Z]
+    a_z = []
+    for g in range(2):
+        for d in range(1, CY):
+            a_y[d, g].wait_recv()
+        part = pl.ds(32 * g, 32)
+        zin[part, :] = hsum[pl.ds(pl.multiple_of(y * 64 + 32 * g, 32), 32), :] + ybuf[0, part, :] + ybuf[1, part, :] + ybuf[2, part, :]
+        for pos in range(4 * g, 4 * g + 4):
+            d = (FAR_Z + (0,))[pos]
+            if d:
+                a_z.append(send(zin.at[pl.ds(8 * pos, 8), :], zbuf.at[d - 1], A_Z + d, chip(0, d)))
 
     own = rows_of(0, 0)
 
@@ -308,18 +343,31 @@
     for copy in s_y:
         copy.wait_recv()
     szbuf[z] = ssum[block_of(y, 16), :] + sybuf[0] + sybuf[1] + sybuf[2]
-    s_z = [send(szbuf.at[z], szbuf.at[z], S_Z + d, chip(0, d)) for d in FAR_Z]
-
+
+    def small_over_z(d):
+        return remote(szbuf.at[z], szbuf.at[z], S_Z + d, chip(0, d))
+
+    def small_to_root():
+        return remote(szbuf.at[z], szbuf.at[z], S_Z + lax.rem(CZ - z, CZ), (2 * y + 1, x))
+
+    @pl.when(c == 0)
+    def _():
+        for d in FAR_Z:
+            small_over_z(d).start()
+
+    @pl.when((c == 1) & (z > 0))
+    def _():
+        small_to_root().start()
+
+    far = pl.ds(192, 64)
     ring[0].wait_recv()
-    block = gath.at[block_of(lax.rem(x + 3, 4), 64), halves[0]]
-    ring.append(send(block, block, X_RING + 4, right))
+    ring.append(send(gath.at[pl.ds(128, 64), halves[0]], gath.at[far, halves[0]], X_RING + 4, right))
     ring[1].wait_recv()
-    block = gath.at[block_of(lax.rem(x + 1, 4), 64), halves[1]]
-    ring.append(send(block, block, X_RING + 5, left))
+    ring.append(send(gath.at[pl.ds(64, 64), halves[1]], gath.at[far, halves[1]], X_RING + 5, left))
 
     for copy in a_z:
         copy.wait_recv()
-    total = zin[block_of(z, 8), :]
+    total = zin[56:64, :]
     for d in range(1, CZ):
         total = total + zbuf[d - 1]
     piv[own, mine] = total
@@ -332,8 +380,62 @@
             a_gy[d, e] = send(part, part, A_GY + d * CZ + e, chip(d, 0))
 
     a_over_y(0)
+
+    def turn_half(g):
+        span = pl.ds(128 * g, 128)
+        for copy in (ring[3],) if g == 0 else (ring[2], ring[4], ring[5]):
+            copy.wait_recv()
+
+        def turn(i, carry):
+            at = block_of(i, 256)
+            kept = jnp.where(hit[0:1, at] > 0.0, 0.0, gath[span, at])
+            hi, lo = split(kept)
+            pre = dot(both_u[:, span], hi)
+            pre = pre[0:64] + pre[64:128] + dot(both_u[0:64, span], lo)
+            lp[:, at] = pre if g == 0 else lp[:, at] + pre
+            left_ref[at, span] = lo.T
+            left_ref[at, pl.ds(256 + 128 * g, 128)] = hi.T
+            return carry
+
+        lax.fori_loop(0, rows // 256, turn, 0, unroll=8)
+
     by_core(head_over_y)
-    for e in NEAR_Z:
+    for e in NEAR_Z[:4]:
+        a_gz[e].wait_recv()
+        a_over_y(e)
+
+    at_small = block_of(c * CY + y, 16)
+
+    def small_over_y(d):
+        return remote(red.at[at_small, :], red.at[at_small, :], S_GY + d, chip(d, 0))
+
+    def small_to_root_y():
+        return remote(red.at[at_small, :], red.at[at_small, :], S_GY + lax.rem(CY - y, CY), (1, x))
+
+    def small_to_core():
+        part = red.at[block_of(c, 64), :]
+        return remote(part, part, S_GC, sibling)
+
+    @pl.when((c == 0) | (z == 0))
+    def _():
+        for d in range(1, CZ):
+            small_over_z(d).wait_recv()
+        total = szbuf[0]
+        for q in range(1, CZ):
+            total = total + szbuf[q]
+        red[at_small, :] = total
+
+    @pl.when(c == 0)
+    def _():
+        for d in range(1, CY):
+            small_over_y(d).start()
+
+    @pl.when((c == 1) & (z == 0) & (y > 0))
+    def _():
+        small_to_root_y().start()
+
+    turn_half(0)
+    for e in NEAR_Z[4:]:
         a_gz[e].wait_recv()
         a_over_y(e)
     a_gc = []
@@ -344,72 +446,44 @@
         part = piv.at[block_of(lax.rem(y + d, CY), 64), mine]
         a_gc.append(send(part, part, A_GC + d, sibling))
 
-    for copy in s_z:
-        copy.wait_recv()
-    total = szbuf[0]
-    for q in range(1, CZ):
-        total = total + szbuf[q]
-    at_small = block_of(c * CY + y, 16)
-    red[at_small, :] = total
-    s_gy = [send(red.at[at_small, :], red.at[at_small, :], S_GY + d, chip(d, 0)) for d in range(1, CY)]
-
-    loads["upper"].wait()
-    loads["lower"].wait()
-    i = lax.broadcasted_iota(jnp.int32, (NB, NB), 0)
-    j = lax.broadcasted_iota(jnp.int32, (NB, NB), 1)
-    low = split(jnp.where(i > j, low_v[...], jnp.where(i == j, 1.0, 0.0)))
-    up = jnp.where(i <= j, up_v[...], 0.0)
-    low_v[...] = up.T
-    u = split(low_v[own_block, :])
-    both_u = jnp.concatenate(u, 0)
+    by_core(head_over_core)
+
+    @pl.when((c == 0) | (r == 1))
+    def _():
+        for d in range(1, CY):
+            small_over_y(d).wait_recv()
+        small_to_core().start()
+
     for copy in a_gc:
         copy.wait_recv()
-    u_rows = dot3(low, split(piv[...]))
-    ur[...] = u_rows
-    vh, vl = split(dot3(split(up), split(u_rows)))
+    rows_in = split(piv[...])
+    vh, vl = split(dot3((mulh[...], mull[...]), rows_in))
     va[0:256, :] = -vh
     va[256:512, :] = -vh
     vb[0:256, :] = -vl
 
-    by_core(head_over_core)
-
-    for copy in ring[2:]:
-        copy.wait_recv()
-
-    def turn(i, carry):
-        at = block_of(i, 256)
-        kept = jnp.where(hit[0:1, at] > 0.0, 0.0, gath[:, at])
-        hi, lo = split(kept)
-        pre = dot(both_u, hi)
-        lp[:, at] = pre[0:64] + pre[64:128] + dot(u[0], lo)
-        hi, lo = split(kept.T)
-        left_ref[at, 0:256] = lo
-        left_ref[at, 256:512] = hi
-        return carry
-
-    lax.fori_loop(0, rows // 256, turn, 0)
-
-    for copy in s_gy:
-        copy.wait_recv()
-    part = red.at[block_of(c, 64), :]
-    s_gc = send(part, part, S_GC, sibling)
+    @pl.when(r == 0)
+    def _():
+        ur[...] = dot3((lowh[...], lowl[...]), rows_in)
+
+    turn_half(1)
 
     pl.when(c == 0)(lambda: head_arrived(phead))
     pl.when(c == 1)(lambda: head_arrived(head))
-    moved = (head[...] - piv[...]) - dot3(split(phead[...].T), (vh, vl))
+    cols = reorder(phead)
+    moved = (head[...] - piv[...]) - dot3(split(cols.T), (vh, vl))
     dh, dl = split(moved)
     va[512:768, :] = dh
     vb[256:512, :] = dl
-    both_f = jnp.concatenate(split(dot3(u, split(phead[...]))), 0)
-
-    def moved_factor(i, carry):
-        at = block_of(i, 256)
-        add = dot(both_f, hot_t[:, at])
-        lp[:, at] += add[0:64] + add[64:128]
-        return carry
-
-    lax.fori_loop(0, rows // 256, moved_factor, 0)
-    s_gc.wait_recv()
+    both_f = jnp.concatenate(split(dot3((both_u[0:64, :], both_u[64:128, :]), split(cols))), 0)
+
+    add = dot(both_f, hot_t[...])
+    lp[...] += add[0:64] + add[64:128]
+
+    @pl.when((c == 1) | (r == 0))
+    def _():
+        small_to_core().wait_recv()
+
     sk[...] = red[0:64, :]
 
     @pl.when(r == 0)
@@ -419,6 +493,25 @@
     for copy in pending:
         copy.wait_send()
     by_core(head_left)
+
+    @pl.when(c == 0)
+    def _():
+        for d in range(1, CZ):
+            small_over_z(d).wait_send()
+        for d in range(1, CY):
+            small_over_y(d).wait_send()
+
+    @pl.when((c == 1) & (z > 0))
+    def _():
+        small_to_root().wait_send()
+
+    @pl.when((c == 1) & (z == 0) & (y > 0))
+    def _():
+        small_to_root_y().wait_send()
+
+    @pl.when((c == 0) | (r == 1))
+    def _():
+        small_to_core().wait_send()
 
     @pl.when(r == 0)
     def _():
@@ -458,7 +551,7 @@
         write(i).start()
         return carry
 
-    lax.fori_loop(0, steps, step, 0)
+    lax.fori_loop(0, steps, step, 0, unroll=True)
     for copy in small:
         copy.wait()
     for i in range(steps):
@@ -513,6 +606,11 @@
             pltpu.VMEM((3, 16, NB), F32),
             pltpu.VMEM((CZ, 16, NB), F32),
             pltpu.VMEM((128, NB), F32),
+            pltpu.VMEM((NB, NB), BF16),
+            pltpu.VMEM((NB, NB), BF16),
+            pltpu.VMEM((NB, NB), BF16),
+            pltpu.VMEM((NB, NB), BF16),
+            pltpu.VMEM((128, NB), BF16),
             pltpu.SemaphoreType.DMA((8,)),
             pltpu.SemaphoreType.DMA((N_SEM,)),
             pltpu.SemaphoreType.DMA((N_SEM,)),

time: 49.3 us -> 44.2 us (0.90)
  Pallas kernels: 48.5 us -> 43.5 us
    pallas_call x1, Pallas kernels: 43.6 us -> 39.5 us  [on_device(): pl.pallas_call(exchange_kernel, out_shape=(jax.ShapeDtypeStruct((rows, 3...]
    pallas_call x1, Pallas kernels: 4.93 us -> 4.01 us  [on_device(): pl.pallas_call(update_kernel, out_shape=(jax.ShapeDtypeStruct((rows, widt...]
where the time goes in v4:
time: 44.2 us
  Pallas kernels  43.5 us (98%)
  between operations  0.66 us (1%)
    pallas_call x1, Pallas kernels, on_device(): pl.pallas_call(exchange_kernel, out_shape=(jax.ShapeDtypeStruct((rows, 3...  39.5 us
    pallas_call x1, Pallas kernels, on_device(): pl.pallas_call(update_kernel, out_shape=(jax.ShapeDtypeStruct((rows, widt...  4.01 us

profile of v4, /device:TPU:1, one launch (start us, length us, event | category | flops | bytes accessed | tf_op | source)
XLA Modules:
  0.0 44.2 jit_solution(17553741751218861923)
XLA Ops:
  0.6 0.0 copy-start
  0.6 39.5 %exchange.1 = (bf16[2048,768]{1,0:T(8,128)(2,1)S(1)}, bf16[768,512]{1,0:T(8,128)(2,1)S(1)}, bf16[512,512]{1,0:T(8,128)(2,1)S(1)}, f32[256,512]{1,0:T(8,128)S(1)}...) custom-call(s32[256]{0:T(256)} %pivots.1, s32[1,256]{1,0:T(1,128)} %bitcast.6, f32[64,2048]{1,0:T(8,128)} %bitcast.5, ...), custom_call_target="tpu_custom_call" | custom-call | tf_op jit(solution)/shard_map/exchange/pallas_call | solution.py:571
  40.1 0.0 copy-done
  40.1 4.0 %update.1 = (f32[2048,512]{1,0:T(8,128)}, f32[64,2048]{1,0:T(8,128)}, f32[64,256]{1,0:T(8,128)}) custom-call(s32[1]{0:T(128)} %bitcast.first, f32[2048,512]{1,0:T(8,128)S(1)} %copy-done, bf16[2048,768]{1,0:T(8,128)(2,1)S(1)} %get-tuple-element.12.left_ref, bf16[768,512]{1,0:T(8,128)(2,1)S(1)} %get-tuple-element.13.va, ...), custom_call_target="tpu_custom_call" | custom-call | tf_op jit(solution)/shard_map/update/pallas_call | solution.py:626
Async XLA Ops:
  0.6 39.5 %copy-start = (f32[2048,512]{1,0:T(8,128)S(1)}, f32[2048,512]{1,0:T(8,128)}, u32[]{:S(2)}) copy-start(f32[2048,512]{1,0:T(8,128)} %look.3) | copy-start | bytes 12582916

commit v5 on v4

--- a/solution.py
+++ b/solution.py
@@ -52,7 +52,7 @@
 def exchange_kernel(
     pivots, piv_row, panel, look, smap, upper, lower,
     left_ref, va, vb, ur, lp, sk,
-    piv_s, piv_v, look_v, sm_v, up_v, low_v, gath, hot_t, hit,
+    piv_s, piv_v, look_a, look_b, sm_v, up_v, low_v, gath, hot_t, hit,
     pick, cbuf, hsum, ybuf, zin, zbuf, piv, head, phead, deal,
     spart, scbuf, ssum, sybuf, szbuf, red, lowh, lowl, mulh, mull, both_u,
     ld, ss, rs,
@@ -97,19 +97,16 @@
     halves = [pl.ds(0, half_cols), pl.ds(half_cols, half_cols)]
 
     loads = {}
-    for i, (name, src, dst) in enumerate(
-        (
-            ("piv_s", pivots, piv_s),
-            ("look", look, look_v),
-            ("piv_v", piv_row, piv_v),
-            ("panel", panel, gath.at[pl.ds(0, 64), :]),
-            ("map", smap, sm_v),
-            ("upper", upper, up_v),
-            ("lower", lower, low_v),
-        )
-    ):
-        loads[name] = pltpu.make_async_copy(src, dst, ld.at[i])
+
+    def load(name, src, dst):
+        loads[name] = pltpu.make_async_copy(src, dst, ld.at[len(loads)])
         loads[name].start()
+
+    load("piv_s", pivots, piv_s)
+    load("other", look.at[:, other], look_a)
+    load("mine", look.at[:, mine], look_b)
+    load("piv_v", piv_row, piv_v)
+    load("panel", panel, gath.at[pl.ds(0, 64), :])
 
     bar = pltpu.get_barrier_semaphore()
 
@@ -131,23 +128,24 @@
             greet((0, lax.rem(x + d, 4)))
 
     loads["piv_s"].wait()
-    loads["look"].wait()
-
-    def pick_rows(i, carry):
-        pos = lax.rem(i, CZ)
-        step = lax.div(pos + 1, 2)
-        dz = jnp.where(lax.rem(pos, 2) == 1, 4 - step, 4 + step)
-        start = (lax.div(i, CZ) * CZ + lax.rem(z + dz, CZ)) * 8
-        for k in range(8):
-            row = i * 8 + k
-            local = piv_s[start + k] - first
-            owned = (local >= 0) & (local < rows)
-            at = jnp.where(owned, local, 0)
-            pick[pl.ds(row, 1), :] = jnp.where(owned, look_v[pl.ds(at, 1), :], 0.0)
-        return carry
-
-    lax.fori_loop(0, NB // 8, pick_rows, 0)
-
+
+    def pick_half(half, look_v):
+        def pick_rows(i, carry):
+            pos = lax.rem(i, CZ)
+            step = lax.div(pos + 1, 2)
+            dz = jnp.where(lax.rem(pos, 2) == 1, 4 - step, 4 + step)
+            start = (lax.div(i, CZ) * CZ + lax.rem(z + dz, CZ)) * 8
+            for k in range(8):
+                local = piv_s[start + k] - first
+                owned = (local >= 0) & (local < rows)
+                at = jnp.where(owned, local, 0)
+                pick[half, pl.ds(i * 8 + k, 1), :] = jnp.where(owned, look_v[pl.ds(at, 1), :], 0.0)
+            return carry
+
+        lax.fori_loop(0, NB // 8, pick_rows, 0, unroll=1)
+
+    loads["other"].wait()
+    pick_half(0, look_a)
     extra = (CY - 1) * (CZ - 1)
 
     @pl.when(r == 0)
@@ -165,7 +163,7 @@
     a_core = []
     for d in (2, 1, 3, 0):
         block = block_of(lax.rem(y + d, CY), 64)
-        a_core.append((d, block, send(pick.at[block, other], cbuf.at[block, :], A_CORE + d, sibling)))
+        a_core.append((d, block, send(pick.at[0, block, :], cbuf.at[block, :], A_CORE + d, sibling)))
 
     def share(ref, q):
         return ref.at[block_of(lax.rem(q, CY) * CZ + lax.div(q, CY), 8), :]
@@ -180,7 +178,7 @@
     def columns(to):
         return remote(panel.at[:, pl.ds(0, NB)], deal.at[block_of(x, 64), :], H_X + to, (1, to), H_X + x)
 
-    own_head = pltpu.make_async_copy(look.at[pl.ds(0, 8), :], head.at[pl.ds(0, 8), :], ld.at[7])
+    own_head = pltpu.make_async_copy(look.at[pl.ds(0, 8), :], head.at[pl.ds(0, 8), :], ld.at[8])
 
     @pl.when(r == 0)
     def _():
@@ -197,13 +195,19 @@
         send(panel.at[:, halves[0]], gath.at[pl.ds(64, 64), halves[0]], X_RING + 3, left),
     ]
 
+    load("map", smap, sm_v)
+    load("upper", upper, up_v)
+    load("lower", lower, low_v)
+    loads["mine"].wait()
+    pick_half(1, look_b)
+
     def group(block, g):
         return hsum.at[pl.ds(pl.multiple_of(block * 64 + g * 32, 32), 32), :]
 
     a_y = {}
     for d, block, copy in a_core:
         copy.wait_recv()
-        hsum[block, :] = pick[block, mine] + cbuf[block, :]
+        hsum[block, :] = pick[1, block, :] + cbuf[block, :]
         if d:
             part = group(lax.rem(y + d, CY), 0)
             a_y[d, 0] = send(part, ybuf.at[d - 1, pl.ds(0, 32), :], A_Y + d, chip(d, 0))
@@ -359,12 +363,6 @@
     def _():
         small_to_root().start()
 
-    far = pl.ds(192, 64)
-    ring[0].wait_recv()
-    ring.append(send(gath.at[pl.ds(128, 64), halves[0]], gath.at[far, halves[0]], X_RING + 4, right))
-    ring[1].wait_recv()
-    ring.append(send(gath.at[pl.ds(64, 64), halves[1]], gath.at[far, halves[1]], X_RING + 5, left))
-
     for copy in a_z:
         copy.wait_recv()
     total = zin[56:64, :]
@@ -380,6 +378,13 @@
             a_gy[d, e] = send(part, part, A_GY + d * CZ + e, chip(d, 0))
 
     a_over_y(0)
+
+    far = pl.ds(192, 64)
+    ring[0].wait_recv()
+    ring.append(send(gath.at[pl.ds(128, 64), halves[0]], gath.at[far, halves[0]], X_RING + 4, right))
+    ring[1].wait_recv()
+    ring.append(send(gath.at[pl.ds(64, 64), halves[1]], gath.at[far, halves[1]], X_RING + 5, left))
+
 
     def turn_half(g):
         span = pl.ds(128 * g, 128)
@@ -583,14 +588,15 @@
         scratch_shapes=[
             pltpu.SMEM((NB,), jnp.int32),
             pltpu.VMEM((1, NB), jnp.int32),
-            pltpu.VMEM((rows, width), F32),
+            pltpu.VMEM((rows, 256), F32),
+            pltpu.VMEM((rows, 256), F32),
             pltpu.VMEM((NB, rows), F32),
             pltpu.VMEM((NB, NB), F32),
             pltpu.VMEM((NB, NB), F32),
             pltpu.VMEM((NB, rows), F32),
             pltpu.VMEM((NB, rows), BF16),
             pltpu.VMEM((8, rows), F32),
-            pltpu.VMEM((NB, width), F32),
+            pltpu.VMEM((2, NB, 256), F32),
             pltpu.VMEM((NB, 256), F32),
             pltpu.VMEM((NB, 256), F32),
             pltpu.VMEM((3, 64, 256), F32),
@@ -611,7 +617,7 @@
             pltpu.VMEM((NB, NB), BF16),
             pltpu.VMEM((NB, NB), BF16),
             pltpu.VMEM((128, NB), BF16),
-            pltpu.SemaphoreType.DMA((8,)),
+            pltpu.SemaphoreType.DMA((9,)),
             pltpu.SemaphoreType.DMA((N_SEM,)),
             pltpu.SemaphoreType.DMA((N_SEM,)),
         ],

time: 44.2 us -> 43.9 us (level)
  no operation moved by 1% of the time
where the time goes in v5:
time: 43.9 us
  Pallas kernels  43.2 us (98%)
  between operations  0.66 us (2%)
    pallas_call x1, Pallas kernels, on_device(): pl.pallas_call(exchange_kernel, out_shape=(jax.ShapeDtypeStruct((rows, 3...  39.2 us
    pallas_call x1, Pallas kernels, on_device(): pl.pallas_call(update_kernel, out_shape=(jax.ShapeDtypeStruct((rows, widt...  4.01 us

profile of v5, /device:TPU:1, one launch (start us, length us, event | category | flops | bytes accessed | tf_op | source)
XLA Modules:
  0.0 43.9 jit_solution(17832022206416999357)
XLA Ops:
  0.6 0.0 copy-start
  0.6 39.2 %exchange.1 = (bf16[2048,768]{1,0:T(8,128)(2,1)S(1)}, bf16[768,512]{1,0:T(8,128)(2,1)S(1)}, bf16[512,512]{1,0:T(8,128)(2,1)S(1)}, f32[256,512]{1,0:T(8,128)S(1)}...) custom-call(s32[256]{0:T(256)} %pivots.1, s32[1,256]{1,0:T(1,128)} %bitcast.6, f32[64,2048]{1,0:T(8,128)} %bitcast.5, ...), custom_call_target="tpu_custom_call" | custom-call | tf_op jit(solution)/shard_map/exchange/pallas_call | solution.py:576
  39.8 0.0 copy-done
  39.8 4.0 %update.1 = (f32[2048,512]{1,0:T(8,128)}, f32[64,2048]{1,0:T(8,128)}, f32[64,256]{1,0:T(8,128)}) custom-call(s32[1]{0:T(128)} %bitcast.first, f32[2048,512]{1,0:T(8,128)S(1)} %copy-done, bf16[2048,768]{1,0:T(8,128)(2,1)S(1)} %get-tuple-element.12.left_ref, bf16[768,512]{1,0:T(8,128)(2,1)S(1)} %get-tuple-element.13.va, ...), custom_call_target="tpu_custom_call" | custom-call | tf_op jit(solution)/shard_map/update/pallas_call | solution.py:632
Async XLA Ops:
  0.6 39.2 %copy-start = (f32[2048,512]{1,0:T(8,128)S(1)}, f32[2048,512]{1,0:T(8,128)}, u32[]{:S(2)}) copy-start(f32[2048,512]{1,0:T(8,128)} %look.3) | copy-start | bytes 12582916
